TPU v7x, 32 devices: a whole 2x2x4 slice. The times are simulated.
32 devices in a mesh: table: 16 (over z, x, core), scal: 2 (over y).
Axes of the slice: x: 2, y: 2, z: 4, core: 2. Of those that a mesh axis runs over, the one named last changes fastest.
Arguments:
- cell_coords: float32 [4, 32768], P(None, ('table', 'scal')), may hold values from 0 to 1
- flamelet_table: float32 [65536, 1024], P('table', 'scal'), may hold values from -15 to 15
- owner_shard: int32 [32768, 1], P(('table', 'scal')), may hold values from 0 to 15; in each aligned block of 64 rows (0 to 63, 64 to 127, ...) at most 10 rows name the same one
- local_bin: int32 [32768], P(('table', 'scal')), may hold values from 0 to 4095
Outputs:
- filtered_fields: float32 [32, 256, 128], P(None, ('table', 'scal'))
- x_gradient: float32 [32, 256, 128], P(None, ('table', 'scal'))
Inputs may be any that keep to these rules, and one draw needn't show every extreme that they name: `owner_shard`: in each aligned block of 64 rows (one group of one device's cells) no shard is named by more than 10 rows, a bound that some block reaches.
All inputs are finite; a program needn't handle non-finite values.
Results may differ from a plain program's by a relative error of at most 0.00012.
Values sent between devices are 32-bit elements; how exact they have to be, the bound alone decides.
No kernel may reach another device: no remote copies, remote signals or barrier semaphores. Data moves between devices by JAX's collectives and lax.ppermute only.
A program may use at most 128 MiB of HBM per device.

v0:
```python
import jax
import jax.numpy as jnp
import numpy as np
from jax import lax
from jax.sharding import PartitionSpec as P

SCAL_ALL = 32
K = 32
BX = 8
LG = 8


strength = 0.499


def spline_weights(coords):
    linear = [jnp.stack([1.0 - coords[axis_id], coords[axis_id]]) for axis_id in range(3)]
    frac_last = coords[3]
    square = frac_last * frac_last
    cube = square * frac_last
    remain = 1.0 - frac_last
    cubic = jnp.stack(
        [
            remain * remain * remain / 6.0,
            (3.0 * cube - 6.0 * square + 4.0) / 6.0,
            (-3.0 * cube + 3.0 * square + 3.0 * frac_last + 1.0) / 6.0,
            cube / 6.0,
        ]
    )
    product = (
        linear[0][:, None, None, None, :]
        * linear[1][None, :, None, None, :]
        * linear[2][None, None, :, None, :]
        * cubic[None, None, None, :, :]
    )
    return product.reshape(-1, coords.shape[1])


def thomas_solve(below, middle, above, right_side):
    length = middle.shape[0]
    upper_factor = np.zeros(length)
    solved = np.zeros(right_side.shape)
    for row in range(length):
        if row == 0:
            denom = middle[0]
            solved[0] = right_side[0] / denom
        else:
            denom = middle[row] - below[row] * upper_factor[row - 1]
            solved[row] = (right_side[row] - below[row] * solved[row - 1]) / denom
        upper_factor[row] = above[row] / denom
    for row in range(length - 2, -1, -1):
        solved[row] = solved[row] - upper_factor[row] * solved[row + 1]
    return solved


def filter_table(length):
    positions = np.arange(length)
    offset = positions[None, :] - positions[:, None]
    distance = np.abs(offset)
    interior = (positions >= 3) & (positions <= length - 4)
    coeffs = [
        (11.0 + 10.0 * strength) / 16.0,
        (15.0 + 34.0 * strength) / 64.0,
        (-3.0 + 6.0 * strength) / 32.0,
        (1.0 - 2.0 * strength) / 64.0,
    ]
    band = np.zeros((length, length))
    for reach in range(4):
        band = band + np.where(distance == reach, coeffs[reach], 0.0)
    right_side = np.where(interior[:, None], band, np.where(offset == 0, 1.0, 0.0))
    coupling = np.where(interior, strength, 0.0)
    return thomas_solve(coupling, np.ones(length), coupling, right_side).astype(np.float32)


def derivative_table(length):
    positions = np.arange(length)
    offset = positions[None, :] - positions[:, None]
    distance = np.abs(offset)
    direction = np.sign(offset) * 1.0
    boundary = (positions == 0) | (positions == length - 1)
    second = (positions == 1) | (positions == length - 2)
    interior = ~(boundary | second)
    below_diag = np.where(
        interior, 1.0 / 3.0, np.where(second, 0.25, np.where(positions == length - 1, 2.0, 0.0))
    )
    above_diag = np.where(
        interior, 1.0 / 3.0, np.where(second, 0.25, np.where(positions == 0, 2.0, 0.0))
    )
    inner_rows = direction * (
        np.where(distance == 1, 7.0 / 9.0, 0.0) + np.where(distance == 2, 1.0 / 36.0, 0.0)
    )
    second_rows = direction * np.where(distance == 1, 0.75, 0.0)
    first_row = np.where(
        offset == 0, -2.5, np.where(offset == 1, 2.0, np.where(offset == 2, 0.5, 0.0))
    )
    final_row = np.where(
        offset == 0, 2.5, np.where(offset == -1, -2.0, np.where(offset == -2, -0.5, 0.0))
    )
    right_side = np.where(
        interior[:, None],
        inner_rows,
        np.where(
            second[:, None], second_rows, np.where((positions == 0)[:, None], first_row, final_row)
        ),
    )
    return thomas_solve(below_diag, np.ones(length), above_diag, right_side).astype(np.float32)


def on_device(cell_coords, flamelet_table, owner_shard, local_bin):
    table_count = lax.axis_size("table")
    scal_count = lax.axis_size("scal")
    cell_count = cell_coords.shape[1]
    group_size = cell_count // table_count
    capacity = max(2, 5 * group_size // (2 * table_count))
    slot_count = table_count * table_count * capacity
    group_slots = table_count * capacity
    owners = owner_shard[:, 0].reshape(table_count, group_size)
    matches = (
        owners[:, :, None] == jnp.arange(table_count, dtype=jnp.int32)[None, None, :]
    ).astype(jnp.int32)
    group_rank = jnp.sum((jnp.cumsum(matches, axis=1) - 1) * matches, axis=2)
    local_slot = owners * capacity + group_rank
    slot_ids = jnp.arange(group_slots, dtype=jnp.int32)
    placing = (local_slot[:, :, None] == slot_ids[None, None, :]).astype(jnp.float32)
    payload = jnp.concatenate(
        [local_bin.astype(jnp.float32)[None, :], cell_coords], axis=0
    ).reshape(5, table_count, group_size)
    placed = jnp.einsum("fgc,gcq->fgq", payload, placing, precision=lax.Precision.HIGHEST)
    outgoing = (
        placed.reshape(5, table_count, table_count, capacity)
        .transpose(0, 2, 1, 3)
        .reshape(5, table_count, group_slots)
    )
    received = lax.all_to_all(outgoing, "table", split_axis=1, concat_axis=1, tiled=True).reshape(
        5, slot_count
    )
    shard_piece = lax.all_gather(received, "scal", axis=1, tiled=True)
    weights = spline_weights(shard_piece[1:])
    table_rows = jnp.take(flamelet_table, shard_piece[0].astype(jnp.int32), axis=0)
    table_rows = table_rows.reshape(table_rows.shape[0], -1, K)
    looked = jnp.einsum("nsk,kn->sn", table_rows, weights, precision=lax.Precision.HIGHEST)
    looked = looked.reshape(looked.shape[0], scal_count, slot_count)
    grouped = lax.all_to_all(looked, "scal", split_axis=1, concat_axis=0, tiled=True).reshape(
        SCAL_ALL, table_count, table_count, capacity
    )
    length = BX * table_count
    replies = lax.all_to_all(grouped, "table", split_axis=1, concat_axis=1, tiled=True)
    by_group = replies.transpose(0, 2, 1, 3).reshape(SCAL_ALL, table_count, group_slots)
    values = jnp.einsum("sgq,gcq->sgc", by_group, placing, precision=lax.Precision.HIGHEST).reshape(
        SCAL_ALL, table_count, LG, BX
    )
    pencil = lax.all_to_all(values, "table", split_axis=1, concat_axis=3, tiled=True).reshape(
        SCAL_ALL * LG, length
    )
    filter_op = jnp.asarray(filter_table(length).T)
    derivative_op = jnp.asarray(derivative_table(length).T)
    filtered = jnp.dot(pencil, filter_op, precision=lax.Precision.HIGHEST)
    gradient = jnp.dot(filtered, derivative_op, precision=lax.Precision.HIGHEST)
    return (filtered.reshape(SCAL_ALL, LG, length), gradient.reshape(SCAL_ALL, LG, length))


def solution(mesh):
    return jax.shard_map(
        on_device,
        mesh=mesh,
        in_specs=(
            P(None, ("table", "scal")),
            P("table", "scal"),
            P(("table", "scal"), None),
            P(("table", "scal")),
        ),
        out_specs=(P(None, ("table", "scal"), None), P(None, ("table", "scal"), None)),
        check_vma=False,
    )
```

profile of v0, /device:TPU:0, one launch (start us, length us, event | category | flops | bytes accessed | tf_op | source)
XLA Modules:
  0.0 124.1 jit_solution(12325979634999682645)
XLA Ops:
  0.6 0.5 broadcast.128
  1.1 1.3 %reduce.5 = s32[1024]{0:T(1024)S(1)} reduce(s32[1024,1]{0,1:T(1,128)} %param.8, s32[]{:T(128)} %broadcast.128), dimensions={1}, to_apply=%param.8.reduce_sub_computation.3 | reduce | bytes 8196 | tf_op args[2]
  2.6 1.4 %select_reduce_fusion = s32[16,64]{0,1:T(8,128)S(1)} fusion(s32[16,64]{0,1:T(8,128)S(1)} %copy.53), kind=kOutput, calls=%fused_computation.10 | output fusion | flops 1129472 | bytes 8192 | tf_op jit(solution)/shard_map/jit(cumsum)/reduce_window_sum | solution.py:121
  4.2 0.8 concatenate.9
  5.0 0.7 convert_element_type.26
  5.8 0.5 convolution_bitcast_fusion.1
  6.3 0.4 reshape.102
  6.7 0.2 copy.72
  6.9 0.3 reshape.122
  7.4 14.0 %all_to_all.40 = f32[16,1,800]{2,1,0:T(1,128)S(1)} all-to-all(f32[16,1,800]{2,1,0:T(1,128)S(1)} %reshape.132), channel_id=1, replica_groups=mesh['table'=16,'scal'=2] {'table'}, dimensions={0} | all-to-all | bytes 102400 | tf_op jit(solution)/shard_map/all_to_all | solution.py:134
  21.4 0.5 broadcast.129
  21.9 0.8 reduce.6
  22.9 5.1 %all_gather.3 = f32[5,5120]{1,0:T(8,128)S(1)} all-gather(f32[5,2560]{1,0:T(8,128)S(1)} %reshape.104), channel_id=1, replica_groups=mesh['table'=16,'scal'=2] {'scal'}, dimensions={1}, use_global_device_ids=true | all-gather | bytes 153600 | tf_op jit(solution)/shard_map/all_gather | solution.py:137
  28.2 25.7 %gather_fusion = f32[5120,512]{1,0:T(8,128)} fusion(f32[4096,512]{1,0:T(8,128)} %param.7, s32[5120]{0:T(1024)S(1)} %broadcast_clamp_fusion), kind=kCustom, calls=%fused_computation | custom fusion | bytes 20992000 | tf_op jit(solution)/shard_map/jit(_take)/gather | solution.py:139
  53.9 11.4 %copy.60 = f32[5120,512]{0,1:T(8,128)} copy(f32[5120,512]{1,0:T(8,128)} %gather_fusion) | data formatting | bytes 20971520 | tf_op jit(solution)/shard_map/jit(_take)/gather | solution.py:139
  65.8 0.2 mul.131
  66.1 5.8 %multiply_reduce_fusion = f32[5120,16]{0,1:T(8,128)S(1)} fusion(f32[5120,16,32]{0,2,1:T(8,128)} %bitcast.58, f32[5120,32]{0,1:T(8,128)S(1)} %bitcast.61, pred[5120]{0:T(1024)(128)(4,1)S(1)} %compare_and_fusion), kind=kLoop, calls=%fused_computation.1 | loop fusion | flops 7782400 | bytes 11473920 | tf_op jit(solution)/shard_map/nsk,kn->sn/dot_general | solution.py:141
  71.9 8.1 %all_to_all.41 = f32[16,2,2560]{2,0,1:T(8,128)S(1)} all-to-all(f32[16,2,2560]{2,0,1:T(8,128)S(1)} %bitcast.65), channel_id=1, replica_groups=mesh['table'=16,'scal'=2] {'scal'}, dimensions={1} | all-to-all | bytes 655360 | tf_op jit(solution)/shard_map/all_to_all | solution.py:143
  80.0 5.7 %reshape.106 = f32[32,16,16,10]{3,2,1,0:T(8,128)} reshape(f32[2,16,1,2560]{3,1,0,2:T(8,128)S(1)} %bitcast.64) | data formatting | bytes 655360 | tf_op jit(solution)/shard_map/reshape | solution.py:143
  85.8 3.9 %copy.62 = f32[32,16,16,10]{0,2,3,1:T(8,128)S(1)} copy(f32[32,16,16,10]{3,2,1,0:T(8,128)} %reshape.106) | data formatting | bytes 655360 | tf_op jit(solution)/shard_map/reshape | solution.py:143
  89.7 0.6 reshape.134
  90.3 13.7 %all_to_all.42 = f32[16,1,5120]{2,1,0:T(1,128)S(1)} all-to-all(f32[16,1,5120]{2,1,0:T(1,128)S(1)} %reshape.134), channel_id=1, replica_groups=mesh['table'=16,'scal'=2] {'table'}, dimensions={0} | all-to-all | bytes 655360 | tf_op jit(solution)/shard_map/all_to_all | solution.py:147
  104.0 1.4 %reduce.7 = f32[16,5120]{1,0:T(8,128)S(1)} reduce(f32[16,1,5120]{2,1,0:T(1,128)S(1)} %all_to_all.42, f32[]{:T(128)} %broadcast.129), dimensions={1}, to_apply=%all_to_all.32.reduce_sub_computation | reduce | bytes 655364 | tf_op jit(solution)/shard_map/all_to_all | solution.py:147
  105.4 0.4 reshape.135
  105.8 1.5 %fusion.2 = f32[32,16,64]{2,0,1:T(8,128)S(1)} fusion(f32[32,16,160]{0,1,2:T(8,128)S(1)} %bitcast.59, s32[16,64]{1,0:T(8,128)S(1)} %multiply_add_fusion), kind=kOutput, calls=%fused_computation.4 | convolution fusion | flops 63078400 | bytes 462848 | tf_op jit(solution)/shard_map/sgq,gcq->sgc/dot_general | solution.py:149
  107.6 0.3 reshape.136
  107.9 11.0 %all_to_all.43 = f32[16,1,2048]{2,1,0:T(1,128)S(1)} all-to-all(f32[16,1,2048]{2,1,0:T(1,128)S(1)} %reshape.136), channel_id=1, replica_groups=mesh['table'=16,'scal'=2] {'table'}, dimensions={0} | all-to-all | bytes 262144 | tf_op jit(solution)/shard_map/all_to_all | solution.py:152
  118.9 0.9 reduce.8
  120.1 1.7 %copy.65 = f32[32,1,8,16,8]{4,3,2,0,1:T(8,128)S(1)} copy(f32[32,1,8,16,8]{0,4,2,3,1:T(8,128)S(1)} %bitcast_bitcast_fusion) | data formatting | bytes 262144 | tf_op jit(solution)/shard_map/all_to_all | solution.py:152
  121.8 1.0 reshape.109
  122.9 0.3 fusion.15
  123.2 0.9 convolution_bitcast_fusion
  (32 shorter events, 1.9 us)
Async XLA Ops:
  89.7 33.2 %copy-start.2 = (f32[128,128]{1,0:T(8,128)S(1)}, f32[128,128]{1,0:T(8,128)}, u32[]{:S(2)}) copy-start(f32[128,128]{1,0:T(8,128)} %constant.45.clone) | copy-start | bytes 196612
  89.7 33.4 %copy-start.1 = (f32[128,128]{1,0:T(8,128)S(1)}, f32[128,128]{1,0:T(8,128)}, u32[]{:S(2)}) copy-start(f32[128,128]{1,0:T(8,128)} %constant.46.clone) | copy-start | bytes 196612
  123.2 0.9 copy-start
where the time goes:
time: 125 us; the launch traced here: 124 us
  local copies, waits for them, and re-layouts  54.9 us (44%)
  blocking collectives  51.9 us (42%)
  other arithmetic  13.1 us (10%)
  matrix products  3.2 us (3%)
    gather x2, local copies, waits for them, and re-layouts, on_device(): jnp.take(flamelet_table, shard_piece[0].astype(jnp.int32), axis=0)  37.1 us
    all_to_all x1, blocking collectives, on_device(): lax.all_to_all(outgoing, 'table', split_axis=1, concat_axis=1, tiled=True)  14 us
    all_to_all x1, blocking collectives, on_device(): lax.all_to_all(grouped, 'table', split_axis=1, concat_axis=1, tiled=True)  13.7 us
    all_to_all x1, blocking collectives, on_device(): lax.all_to_all(values, 'table', split_axis=1, concat_axis=3, tiled=True)  11 us
    reshape x2, local copies, waits for them, and re-layouts, on_device(): lax.all_to_all(looked, 'scal', split_axis=1, concat_axis=0, tiled=True)  9.65 us
    all_to_all x1, blocking collectives, on_device(): lax.all_to_all(looked, 'scal', split_axis=1, concat_axis=0, tiled=True)  8.11 us
    dot_general x1, other arithmetic, on_device(): jnp.einsum('nsk,kn->sn', table_rows, weights, precision=lax.Precision.HIG...  5.82 us
    all_gather x1, blocking collectives, on_device(): shard_piece = lax.all_gather(received, 'scal', axis=1, tiled=True)  5.12 us

commit v1 on v0

v1 whole, which is shorter than its diff:
```python
import functools

import jax
import jax.numpy as jnp
import numpy as np
from jax import lax
from jax.experimental import pallas as pl
from jax.experimental.pallas import tpu as pltpu
from jax.sharding import PartitionSpec as P

SCAL_ALL = 32
K = 32
BX = 8
LG = 8
GROUP = BX * LG
LANES = 128
AXES = ("table", "scal")

strength = 0.499


def thomas_solve(below, middle, above, right_side):
    length = middle.shape[0]
    upper_factor = np.zeros(length)
    solved = np.zeros(right_side.shape)
    for row in range(length):
        if row == 0:
            denom = middle[0]
            solved[0] = right_side[0] / denom
        else:
            denom = middle[row] - below[row] * upper_factor[row - 1]
            solved[row] = (right_side[row] - below[row] * solved[row - 1]) / denom
        upper_factor[row] = above[row] / denom
    for row in range(length - 2, -1, -1):
        solved[row] = solved[row] - upper_factor[row] * solved[row + 1]
    return solved


def filter_table(length):
    positions = np.arange(length)
    offset = positions[None, :] - positions[:, None]
    distance = np.abs(offset)
    interior = (positions >= 3) & (positions <= length - 4)
    coeffs = [
        (11.0 + 10.0 * strength) / 16.0,
        (15.0 + 34.0 * strength) / 64.0,
        (-3.0 + 6.0 * strength) / 32.0,
        (1.0 - 2.0 * strength) / 64.0,
    ]
    band = np.zeros((length, length))
    for reach in range(4):
        band = band + np.where(distance == reach, coeffs[reach], 0.0)
    right_side = np.where(interior[:, None], band, np.where(offset == 0, 1.0, 0.0))
    coupling = np.where(interior, strength, 0.0)
    return thomas_solve(coupling, np.ones(length), coupling, right_side)


def derivative_table(length):
    positions = np.arange(length)
    offset = positions[None, :] - positions[:, None]
    distance = np.abs(offset)
    direction = np.sign(offset) * 1.0
    boundary = (positions == 0) | (positions == length - 1)
    second = (positions == 1) | (positions == length - 2)
    interior = ~(boundary | second)
    below_diag = np.where(
        interior, 1.0 / 3.0, np.where(second, 0.25, np.where(positions == length - 1, 2.0, 0.0))
    )
    above_diag = np.where(
        interior, 1.0 / 3.0, np.where(second, 0.25, np.where(positions == 0, 2.0, 0.0))
    )
    inner_rows = direction * (
        np.where(distance == 1, 7.0 / 9.0, 0.0) + np.where(distance == 2, 1.0 / 36.0, 0.0)
    )
    second_rows = direction * np.where(distance == 1, 0.75, 0.0)
    first_row = np.where(
        offset == 0, -2.5, np.where(offset == 1, 2.0, np.where(offset == 2, 0.5, 0.0))
    )
    final_row = np.where(
        offset == 0, 2.5, np.where(offset == -1, -2.0, np.where(offset == -2, -0.5, 0.0))
    )
    right_side = np.where(
        interior[:, None],
        inner_rows,
        np.where(
            second[:, None], second_rows, np.where((positions == 0)[:, None], first_row, final_row)
        ),
    )
    return thomas_solve(below_diag, np.ones(length), above_diag, right_side)


class Plan:
    def __init__(self, table, scal, cells):
        self.table, self.scal, self.cells = table, scal, cells
        self.devices = table * scal
        self.cap = max(2, 5 * GROUP // (2 * table))
        self.near = LANES // table
        self.far = self.cap - self.near
        self.quad = 4 * self.far
        assert cells == table * GROUP and table * self.quad == LANES
        self.code = 1 << (self.cap - 1).bit_length()
        self.scalars = SCAL_ALL // scal
        self.cols = self.scalars * K // LANES
        self.few = self.scalars // 4
        self.rows = self.scalars + self.few
        self.nx = BX * table


def iota(shape, dim):
    return lax.broadcasted_iota(jnp.int32, shape, dim)


def pieces_of(values, count):
    pieces = []
    for _ in range(count - 1):
        piece = values.astype(jnp.bfloat16)
        pieces.append(piece)
        values = values - piece.astype(jnp.float32)
    pieces.append(values.astype(jnp.bfloat16))
    return pieces


def dot_rows(a, b):
    return lax.dot_general(a, b, (((1,), (1,)), ((), ())), preferred_element_type=jnp.float32)


def request_kernel(plan, coords_ref, owner_ref, bin_ref, out_ref, x_ref):
    p = plan
    row_count = p.cells // LANES
    half = iota((1, LANES), 1) // GROUP
    shard_ids = iota((p.table, LANES), 0)
    owners = owner_ref[...]
    bins = bin_ref[...]
    address = ((bins >> 3) * (8 * p.cols) + (bins & 7)).astype(jnp.float32)
    hits = [owners[i : i + 1, :] == shard_ids for i in range(row_count)]
    before = iota((LANES, LANES), 0)
    after = iota((LANES, LANES), 1)
    earlier = ((before < after) & (before // GROUP == after // GROUP)).astype(jnp.bfloat16)
    ones = jnp.concatenate([h.astype(jnp.float32) for h in hits], axis=0)
    counts = jnp.dot(ones.astype(jnp.bfloat16), earlier, preferred_element_type=jnp.float32)
    x_ref[0:4, :] = coords_ref[...]
    x_ref[5:8, :] = jnp.zeros((3, p.cells), jnp.float32)
    for i in range(row_count):
        x_ref[4:5, i * LANES : (i + 1) * LANES] = address[i : i + 1, :]
    lane_rows = iota((LANES, LANES), 0)
    left, right, codes = [], [], []
    for i in range(row_count):
        span = slice(i * p.table, (i + 1) * p.table)
        rank = jnp.sum(ones[span] * counts[span], axis=0, keepdims=True).astype(jnp.int32)
        codes.append((owners[i : i + 1, :] * p.code + rank).astype(jnp.float32))
        group = 2 * i + half
        near = jnp.where(rank < p.near, group * p.near + rank, -1)
        far = jnp.where(rank >= p.near, group * p.far + rank - p.near, -1)
        right.append(
            jnp.concatenate(
                [
                    (lane_rows == near).astype(jnp.float32),
                    (lane_rows % 32 == far).astype(jnp.float32),
                ],
                axis=0,
            ).astype(jnp.bfloat16)
        )
        fields = x_ref[:, i * LANES : (i + 1) * LANES]
        chosen = jnp.where(hits[i][:, None, :], fields[None], 0.0).reshape(p.table * 8, LANES)
        left.append(jnp.concatenate(pieces_of(chosen, 3), axis=0))
    placed = dot_rows(jnp.concatenate(left, axis=1), jnp.concatenate(right, axis=1))
    total = p.table * 8
    placed = placed[0:total] + placed[total : 2 * total] + placed[2 * total :]
    sub = iota((8, LANES), 0)
    block = iota((8, LANES), 1) // 32
    for o in range(p.table):
        near_part = placed[o * 8 : (o + 1) * 8, :LANES]
        far_part = placed[o * 8 : (o + 1) * 8, LANES:]
        far_coords = jnp.sum(jnp.where(sub == block, far_part, 0.0), axis=0, keepdims=True)
        message = jnp.where(
            sub < 5,
            near_part,
            jnp.where(sub == 5, far_coords, jnp.where(sub == 6, far_part[4:5], codes[o // 2])),
        )
        for sc in range(p.scal):
            out_ref[o * p.scal + sc] = message


def spline_rows(f):
    shape = (K, f[0].shape[1])
    k = iota(shape, 0)
    product = None
    for axis, bit in ((0, 16), (1, 8), (2, 4)):
        factor = jnp.where((k & bit) != 0, f[axis], 1.0 - f[axis])
        product = factor if product is None else product * factor
    last = f[3]
    square = last * last
    cube = square * last
    remain = 1.0 - last
    basis = [
        remain * remain * remain / 6.0,
        (3.0 * cube - 6.0 * square + 4.0) / 6.0,
        (-3.0 * cube + 3.0 * square + 3.0 * last + 1.0) / 6.0,
        cube / 6.0,
    ]
    d = k & 3
    cubic = jnp.where(d == 0, basis[0], jnp.where(d == 1, basis[1], jnp.where(d == 2, basis[2], basis[3])))
    return product * cubic


def lookup_kernel(
    plan, recv_ref, table_ref, out_ref, ints_ref, near_idx, far_idx, w_near, w_far, sem, *gathered
):
    p = plan
    ints_ref[0] = recv_ref[pl.ds(4, p.devices, stride=8), :].astype(jnp.int32)
    ints_ref[1] = recv_ref[pl.ds(6, p.devices, stride=8), :].astype(jnp.int32)
    copies = [
        pltpu.make_async_copy(ints_ref.at[0], near_idx, sem.at[0]),
        pltpu.make_async_copy(ints_ref.at[1], far_idx, sem.at[1]),
    ]
    for copy in copies:
        copy.start()

    lane = iota((1, LANES), 1)
    spread = (iota((3 * K, LANES), 0) % K == iota((3 * K, LANES), 1) % K).astype(jnp.float32)
    spread = spread.astype(jnp.bfloat16)

    def weigh(u, carry):
        blocks = [
            recv_ref[pl.ds(pl.multiple_of((4 * u + i) * 8, 8), 8), :] for i in range(4)
        ]
        parts = [spline_rows([block[f : f + 1, :] for f in range(4)]) for block in blocks]
        far = []
        for f in range(4):
            row = jnp.zeros((1, LANES), jnp.float32)
            for i in range(4):
                turned = pltpu.roll(blocks[i][5:6, :], (32 * (i - f)) % LANES, 1)
                row = jnp.where(lane // 32 == i, turned, row)
            far.append(row)
        parts.append(spline_rows(far))
        rows = jnp.concatenate(parts, axis=1)
        rows = jnp.concatenate(pieces_of(rows, 3), axis=0)
        weights = lax.dot_general(
            rows, spread, (((0,), (0,)), ((), ())), preferred_element_type=jnp.float32
        )
        for i in range(4):
            src = 4 * u + i
            t, s = src // p.scal, src % p.scal
            for g in range(p.table):
                start = (g * p.scal + s) * LANES + t * p.near
                w_near[pl.ds(pl.multiple_of(start, p.near), p.near), :] = weights[
                    i * LANES + g * p.near : i * LANES + (g + 1) * p.near
                ]
            for q in range(p.table // 4):
                start = (q * p.scal + s) * LANES + t * p.quad
                row = 4 * LANES + 32 * i + q * p.quad
                w_far[pl.ds(pl.multiple_of(start, p.quad), p.quad), :] = weights[row : row + p.quad]
        return carry

    lax.fori_loop(0, p.devices // 4, weigh, 0)
    for copy in copies:
        copy.wait()

    depth = p.cols * LANES
    choose = (iota((p.scalars, depth), 0) == iota((p.scalars, depth), 1) // K).astype(jnp.float32)
    choose = jnp.concatenate([choose.astype(jnp.bfloat16)] * 2, axis=1)

    def fetch(store, slot, address):
        if p.cols == 1:
            store[pl.ds(slot, 1), :] = table_ref[pl.ds(address, 1), :]
        else:
            store[pl.ds(slot, p.cols, stride=LANES), :] = table_ref[
                pl.ds(address, p.cols, stride=8), :
            ]

    def reduce(store, weights):
        high, low = [], []
        for c in range(p.cols):
            product = store[c * LANES : (c + 1) * LANES, :] * weights
            two = pieces_of(product, 2)
            high.append(two[0])
            low.append(two[1])
        return dot_rows(choose, jnp.concatenate(high + low, axis=1))

    def near_chunks(g, carry):
        for s in range(p.scal):
            for t in range(p.table):
                for q in range(p.near):
                    fetch(gathered[s], t * p.near + q, near_idx[t * p.scal + s, g * p.near + q])
        for s in range(p.scal):
            dest = g * p.scal + s
            weights = w_near[pl.ds(pl.multiple_of(dest * LANES, LANES), LANES), :]
            out_ref[pl.ds(dest * p.rows, p.scalars), :] = reduce(gathered[s], weights)
        return carry

    lax.fori_loop(0, p.table, near_chunks, 0)
    quad_of = (lane // p.far) % 4

    def far_chunks(quad, carry):
        for s in range(p.scal):
            for t in range(p.table):
                for q in range(p.quad):
                    fetch(gathered[s], t * p.quad + q, far_idx[t * p.scal + s, quad * p.quad + q])
        for s in range(p.scal):
            chunk = quad * p.scal + s
            weights = w_far[pl.ds(pl.multiple_of(chunk * LANES, LANES), LANES), :]
            tile = reduce(gathered[s], weights)
            for i in range(4):
                message = jnp.zeros((p.few, LANES), jnp.float32)
                for b in range(4):
                    turned = pltpu.roll(
                        tile[b * p.few : (b + 1) * p.few], ((b - i) * p.far) % LANES, 1
                    )
                    message = jnp.where(quad_of == b, turned, message)
                dest = (quad * 4 + i) * p.scal + s
                out_ref[pl.ds(dest * p.rows + p.scalars, p.few), :] = message
        return carry

    lax.fori_loop(0, p.table // 4, far_chunks, 0)


def slots_kernel(plan, me_ref, recv_ref, out_ref):
    p = plan
    table_at, scal_at = me_ref[0], me_ref[1]
    width = LG * p.nx
    codes = recv_ref[pl.ds(scal_at * 8 + 7, p.table, stride=8 * p.scal), :]
    cell = iota((LANES, width), 1)
    inside = (cell // p.nx) * BX + cell % BX + GROUP * (table_at % 2)
    move = (iota((LANES, width), 0) == inside).astype(jnp.float32).astype(jnp.bfloat16)
    moved = jnp.dot(codes.astype(jnp.bfloat16), move, preferred_element_type=jnp.float32)
    x_block = (iota((p.table, width), 1) % p.nx) // BX
    moved = jnp.where(iota((p.table, width), 0) == x_block, moved, 0.0)
    code = jnp.sum(moved, axis=0, keepdims=True).astype(jnp.int32)
    shard, slot = code // p.code, code % p.code
    t = (iota((1, width), 1) % p.nx) // BX
    near = jnp.where(slot < p.near, shard * LANES + t * p.near + slot, -1)
    far = jnp.where(
        slot >= p.near,
        (shard // 4 + p.table) * LANES + t * p.quad + (shard % 4) * p.far + slot - p.near,
        -1,
    )
    chosen = jnp.where(slot < p.near, near, far)
    step = 2 * LANES
    rows = iota((step, width), 0)

    def fill(i, carry):
        start = pl.multiple_of(i * step, step)
        hit = rows == chosen - start
        out_ref[pl.ds(start, step), :] = jnp.where(hit, 1.0, 0.0).astype(jnp.bfloat16)
        return carry

    lax.fori_loop(0, out_ref.shape[0] // step, fill, 0)


def filter_kernel(plan, recv_ref, place_ref, op_ref, filtered_ref, gradient_ref, left_ref):
    p = plan
    lane = iota((1, LANES), 1)
    quad_of = (lane // p.far) % 4
    for o in range(p.table):
        for sc in range(p.scal):
            start = (o * p.scal + sc) * p.rows
            left_ref[sc * p.scalars : (sc + 1) * p.scalars, o * LANES : (o + 1) * LANES] = recv_ref[
                start : start + p.scalars, :
            ]
    for quad in range(p.table // 4):
        for sc in range(p.scal):
            messages = []
            for i in range(4):
                start = ((quad * 4 + i) * p.scal + sc) * p.rows + p.scalars
                messages.append(recv_ref[start : start + p.few, :])
            for b in range(4):
                part = jnp.zeros((p.few, LANES), jnp.float32)
                for i in range(4):
                    turned = pltpu.roll(messages[i], ((i - b) * p.far) % LANES, 1)
                    part = jnp.where(quad_of == i, turned, part)
                row = sc * p.scalars + b * p.few
                col = (p.table + quad) * LANES
                left_ref[row : row + p.few, col : col + LANES] = part
    left = jnp.concatenate(pieces_of(left_ref[...], 3), axis=0)
    values = jnp.dot(left, place_ref[...], preferred_element_type=jnp.float32)
    values = values[0:SCAL_ALL] + values[SCAL_ALL : 2 * SCAL_ALL] + values[2 * SCAL_ALL :]
    lines = jnp.concatenate(
        [values[:, r * p.nx : (r + 1) * p.nx] for r in range(LG)], axis=0
    )
    both = jnp.dot(
        lines, op_ref[...], precision=lax.Precision.HIGHEST, preferred_element_type=jnp.float32
    )
    for r in range(LG):
        rows = slice(r * SCAL_ALL, (r + 1) * SCAL_ALL)
        filtered_ref[:, r, :] = both[rows, : p.nx]
        gradient_ref[:, r, :] = both[rows, p.nx :]


VMEM = pl.BlockSpec(memory_space=pltpu.VMEM)
SMEM = pl.BlockSpec(memory_space=pltpu.SMEM)


def call(kernel, plan, out_shape, in_specs, scratch, limit, cost, name):
    many = isinstance(out_shape, tuple)
    return pl.pallas_call(
        functools.partial(kernel, plan),
        out_shape=out_shape,
        in_specs=in_specs,
        out_specs=(VMEM,) * len(out_shape) if many else VMEM,
        scratch_shapes=scratch,
        compiler_params=pltpu.CompilerParams(vmem_limit_bytes=limit << 20),
        cost_estimate=pl.CostEstimate(flops=cost, bytes_accessed=cost // 256, transcendentals=0),
        name=name,
    )


def exchange(array):
    return lax.all_to_all(array, AXES, split_axis=0, concat_axis=0, tiled=True)


def on_device(plan, cell_coords, flamelet_table, owner_shard, local_bin):
    p = plan
    f32, i32 = jnp.float32, jnp.int32
    row_count = p.cells // LANES
    owners = owner_shard.reshape(row_count, LANES)
    bins = local_bin.reshape(row_count, LANES)
    requests = call(
        request_kernel,
        p,
        jax.ShapeDtypeStruct((p.devices, 8, LANES), f32),
        [VMEM] * 3,
        [pltpu.VMEM((8, p.cells), f32)],
        32,
        1 << 20,
        "requests",
    )(cell_coords, owners, bins)
    received = exchange(requests).reshape(p.devices * 8, LANES)

    bin_count, depth = flamelet_table.shape
    table = flamelet_table.reshape(bin_count // 8, 8, p.cols, LANES).transpose(0, 2, 1, 3)
    table = table.reshape(bin_count * p.cols, LANES)
    replies = call(
        lookup_kernel,
        p,
        jax.ShapeDtypeStruct((p.devices * p.rows, LANES), f32),
        [VMEM] * 2,
        [
            pltpu.VMEM((2, p.devices, LANES), i32),
            pltpu.SMEM((p.devices, LANES), i32),
            pltpu.SMEM((p.devices, LANES), i32),
            pltpu.VMEM((p.devices * LANES, LANES), f32),
            pltpu.VMEM((p.devices * LANES // 4, LANES), f32),
            pltpu.SemaphoreType.DMA((2,)),
        ]
        + [pltpu.VMEM((p.cols * LANES, LANES), f32) for _ in range(p.scal)],
        48,
        1 << 24,
        "lookup",
    )(received, table)
    answers = exchange(replies.reshape(p.devices, 1, p.rows * LANES))
    answers = answers.reshape(p.devices * p.rows, LANES)

    me = jnp.stack([lax.axis_index("table"), lax.axis_index("scal")]).astype(i32)
    place = call(
        slots_kernel,
        p,
        jax.ShapeDtypeStruct((p.table * 5 * LANES // 4, LG * p.nx), jnp.bfloat16),
        [SMEM, VMEM],
        [],
        48,
        1 << 24,
        "slots",
    )(me, received)
    filter_op = filter_table(p.nx).T
    both_op = np.concatenate([filter_op, filter_op @ derivative_table(p.nx).T], axis=1)
    out = jax.ShapeDtypeStruct((SCAL_ALL, LG, p.nx), f32)
    return call(
        filter_kernel,
        p,
        (out, out),
        [VMEM] * 3,
        [pltpu.VMEM((SCAL_ALL, p.table * 5 * LANES // 4), f32)],
        48,
        1 << 24,
        "filter",
    )(answers, place, jnp.asarray(both_op.astype(np.float32)))


def solution(mesh):
    table, scal = mesh.shape["table"], mesh.shape["scal"]

    def step(cell_coords, flamelet_table, owner_shard, local_bin):
        plan = Plan(table, scal, cell_coords.shape[1])
        return on_device(plan, cell_coords, flamelet_table, owner_shard, local_bin)

    return jax.shard_map(
        step,
        mesh=mesh,
        in_specs=(
            P(None, AXES),
            P("table", "scal"),
            P(AXES, None),
            P(AXES),
        ),
        out_specs=(P(None, AXES, None), P(None, AXES, None)),
        check_vma=False,
    )
```

time: 125 us -> 59.6 us (0.48)
  local copies, waits for them, and re-layouts: 54.9 us -> 6.91 us
  blocking collectives: 51.9 us -> 15.7 us
  Pallas kernels: 0 us -> 25.7 us
  other arithmetic: 13.1 us -> 0.08 us
  waiting for transfers between devices: 0 us -> 7.46 us
  matrix products: 3.2 us -> 0 us
  starting transfers between devices: 0 us -> 2.61 us
    gather x2 -> x0, local copies, waits for them, and re-layouts: 37.1 us -> none  [on_device(): jnp.take(flamelet_table, shard_piece[0].astype(jnp.int32), axis=0)]
    all_to_all x4 -> x1, blocking collectives: 46.8 us -> 15.7 us  [exchange(): return lax.all_to_all(array, AXES, split_axis=0, concat_axis=0, tiled=True)]
    pallas_call x0 -> x4, Pallas kernels: none -> 25.7 us  [the longest x1 21.1 us: on_device(): call(lookup_kernel, p, jax.ShapeDtypeStruct((p.devices * p.rows, LANES),...]
    reshape x8 -> x0, local copies, waits for them, and re-layouts: 11.7 us -> none  [the longest x2 9.65 us: on_device(): lax.all_to_all(looked, 'scal', split_axis=1, concat_axis=0, tiled=True)]
    all_to_all x0 -> x1, waiting for transfers between devices: none -> 7.46 us  [exchange(): return lax.all_to_all(array, AXES, split_axis=0, concat_axis=0, tiled=True)]
    dot_general x1 -> x0, other arithmetic: 5.82 us -> none  [on_device(): jnp.einsum('nsk,kn->sn', table_rows, weights, precision=lax.Precision.HIG...]
    all_gather x1 -> x0, blocking collectives: 5.12 us -> none  [on_device(): shard_piece = lax.all_gather(received, 'scal', axis=1, tiled=True)]
    unnamed x14 -> x12, local copies, waits for them, and re-layouts: 2.18 us -> 6.91 us
  transfers between devices with their start and end apart: 0 -> 1, of which waited for: 0 -> 1; matrix products, arithmetic and copies ran while one was open for 0% -> 0% of each run, Pallas kernels for 0% -> 3%
where the time goes in v1:
time: 59.6 us; the launch traced here: 59.2 us
  Pallas kernels  25.7 us (43%)
  blocking collectives  15.7 us (26%)
  waiting for transfers between devices  7.46 us (13%)
  local copies, waits for them, and re-layouts  6.91 us (12%)
  starting transfers between devices  2.61 us (4%)
  between operations  0.69 us (1%)
    pallas_call x1, Pallas kernels, on_device(): call(lookup_kernel, p, jax.ShapeDtypeStruct((p.devices * p.rows, LANES),...  21.1 us
    all_to_all x1, blocking collectives, exchange(): return lax.all_to_all(array, AXES, split_axis=0, concat_axis=0, tiled=True)  15.7 us
    all_to_all x1, waiting for transfers between devices, exchange(): return lax.all_to_all(array, AXES, split_axis=0, concat_axis=0, tiled=True)  7.46 us
    unnamed x12, local copies, waits for them, and re-layouts  6.91 us
    all_to_all x1, starting transfers between devices, exchange(): return lax.all_to_all(array, AXES, split_axis=0, concat_axis=0, tiled=True)  2.61 us
    pallas_call x1, Pallas kernels, on_device(): call(filter_kernel, p, (out, out), [VMEM] * 3, [pltpu.VMEM((SCAL_ALL, p.t...  2.05 us
    pallas_call x1, Pallas kernels, on_device(): call(slots_kernel, p, jax.ShapeDtypeStruct((p.table * 5 * LANES // 4, LG...  1.87 us
  transfers between devices with their start and end apart: 1, of which 1 were waited for; matrix products, arithmetic and copies ran while one was open for 0% of the time, Pallas kernels for 3%

profile of v1, /device:TPU:0, one launch (start us, length us, event | category | flops | bytes accessed | tf_op | source)
XLA Modules:
  0.0 59.2 jit_solution(9697378721612074822)
XLA Ops:
  0.6 0.0 copy-start.2
  0.6 0.0 copy-start.3
  0.7 0.7 %copy-done.3 = f32[4,1024]{1,0:T(4,128)S(1)} copy-done((f32[4,1024]{1,0:T(4,128)S(1)}, f32[4,1024]{1,0:T(4,128)}, u32[]{:S(2)}) %copy-start.3) | copy-done | bytes 16408
  1.4 0.0 copy-start.4
  1.4 0.7 %copy-done.4 = s32[1024,1]{0,1:T(1,128)S(1)} copy-done((s32[1024,1]{0,1:T(1,128)S(1)}, s32[1024,1]{0,1:T(1,128)}, u32[]{:S(2)}) %copy-start.4) | copy-done | bytes 4120
  2.1 0.0 copy-start.5
  2.1 0.7 %copy-done.5 = s32[1024]{0:T(1024)S(1)} copy-done((s32[1024]{0:T(1024)S(1)}, s32[1024]{0:T(1024)}, u32[]{:S(2)}) %copy-start.5) | copy-done | bytes 4120
  2.8 0.7 %requests.1 = f32[32,8,128]{2,1,0:T(8,128)S(1)} custom-call(f32[4,1024]{1,0:T(4,128)S(1)} %copy-done.3, s32[8,128]{1,0:T(8,128)S(1)} %bitcast.15, s32[8,128]{1,0:T(8,128)S(1)} %bitcast.16), custom_call_target="tpu_custom_call" | custom-call | flops 1048576 | bytes 4096 | tf_op jit(solution)/shard_map/requests/pallas_call | solution.py:417
  3.5 15.7 %all_to_all.10 = f32[32,8,128]{2,1,0:T(8,128)S(1)} all-to-all(f32[32,8,128]{2,1,0:T(8,128)S(1)} %requests.1), channel_id=1, replica_groups=mesh['table'=16,'scal'=2] {'table','scal'}, dimensions={0} | all-to-all | bytes 262144 | tf_op jit(solution)/shard_map/all_to_all | solution.py:408
  19.2 21.1 %lookup.1 = f32[640,128]{1,0:T(8,128)} custom-call(f32[256,128]{1,0:T(8,128)S(1)} %bitcast.13, f32[16384,128]{1,0:T(8,128)} %bitcast.17), custom_call_target="tpu_custom_call" | custom-call | flops 16777216 | bytes 65536 | tf_op jit(solution)/shard_map/lookup/pallas_call | solution.py:432
  40.3 2.6 %all-to-all-start.1 = ((f32[32,1,2560]{2,1,0:T(1,128)}), f32[32,1,2560]{2,1,0:T(1,128)S(1)}, u32[]{:S(2)}, u32[]{:S(2)}) async-start(f32[32,1,2560]{2,1,0:T(1,128)} %bitcast.6), calls=%async_computation.1 | async-start | bytes 655360 | tf_op jit(solution)/shard_map/all_to_all | solution.py:408
  42.9 0.1 pad_add_fusion.me_ref
  43.0 1.9 %slots.1.place_ref = bf16[2560,1024]{1,0:T(8,128)(2,1)S(1)} custom-call(s32[2]{0:T(128)S(1)} %pad_add_fusion.me_ref, f32[256,128]{1,0:T(8,128)S(1)} %bitcast.14), custom_call_target="tpu_custom_call" | custom-call | flops 16777216 | bytes 65536 | tf_op jit(solution)/shard_map/slots/pallas_call | solution.py:454
  44.9 0.0 copy-start
  44.9 2.3 %copy-done = bf16[2560,1024]{1,0:T(8,128)(2,1)} copy-done((bf16[2560,1024]{1,0:T(8,128)(2,1)}, bf16[2560,1024]{1,0:T(8,128)(2,1)S(1)}, u32[]{:S(2)}) %copy-start) | copy-done | bytes 5242904
  47.2 7.5 %all-to-all-done.1 = f32[32,1,2560]{2,1,0:T(1,128)S(1)} async-done(((f32[32,1,2560]{2,1,0:T(1,128)}), f32[32,1,2560]{2,1,0:T(1,128)S(1)}, u32[]{:S(2)}, u32[]{:S(2)}) %all-to-all-start.1) | async-done | bytes 327712 | tf_op jit(solution)/shard_map/all_to_all | solution.py:408
  54.7 0.0 copy-done.2
  54.7 0.0 copy-start.1
  54.7 2.5 %copy-done.1 = bf16[2560,1024]{1,0:T(8,128)(2,1)S(1)} copy-done((bf16[2560,1024]{1,0:T(8,128)(2,1)S(1)}, bf16[2560,1024]{1,0:T(8,128)(2,1)}, u32[]{:S(2)}) %copy-start.1) | copy-done | bytes 5242904
  57.2 2.1 %filter.1 = (f32[32,8,128]{2,1,0:T(8,128)}, f32[32,8,128]{2,1,0:T(8,128)}) custom-call(f32[640,128]{1,0:T(8,128)S(1)} %bitcast.12, bf16[2560,1024]{1,0:T(8,128)(2,1)S(1)} %copy-done.1, f32[128,256]{1,0:T(8,128)S(1)} %copy-done.2), custom_call_target="tpu_custom_call" | custom-call | flops 16777216 | bytes 65536 | tf_op jit(solution)/shard_map/filter/pallas_call | solution.py:467
Async XLA Ops:
  0.6 54.0 %copy-start.2 = (f32[128,256]{1,0:T(8,128)S(1)}, f32[128,256]{1,0:T(8,128)}, u32[]{:S(2)}) copy-start(f32[128,256]{1,0:T(8,128)} %constant.10.clone.op_ref) | copy-start | bytes 393220
  0.6 0.8 %copy-start.3 = (f32[4,1024]{1,0:T(4,128)S(1)}, f32[4,1024]{1,0:T(4,128)}, u32[]{:S(2)}) copy-start(f32[4,1024]{1,0:T(4,128)} %coords_ref.1) | copy-start | bytes 49156
  1.4 0.7 %copy-start.4 = (s32[1024,1]{0,1:T(1,128)S(1)}, s32[1024,1]{0,1:T(1,128)}, u32[]{:S(2)}) copy-start(s32[1024,1]{0,1:T(1,128)} %param.7) | copy-start | bytes 12292
  2.1 0.7 %copy-start.5 = (s32[1024]{0:T(1024)S(1)}, s32[1024]{0:T(1024)}, u32[]{:S(2)}) copy-start(s32[1024]{0:T(1024)} %param.8) | copy-start | bytes 12292
  40.3 14.3 %all-to-all-start.1 = ((f32[32,1,2560]{2,1,0:T(1,128)}), f32[32,1,2560]{2,1,0:T(1,128)S(1)}, u32[]{:S(2)}, u32[]{:S(2)}) async-start(f32[32,1,2560]{2,1,0:T(1,128)} %bitcast.6), calls=%async_computation.1 | async-start | bytes 655360 | tf_op jit(solution)/shard_map/all_to_all | solution.py:408
  44.9 2.3 %copy-start = (bf16[2560,1024]{1,0:T(8,128)(2,1)}, bf16[2560,1024]{1,0:T(8,128)(2,1)S(1)}, u32[]{:S(2)}) copy-start(bf16[2560,1024]{1,0:T(8,128)(2,1)S(1)} %slots.1.place_ref) | copy-start | bytes 15728644
  54.7 2.5 %copy-start.1 = (bf16[2560,1024]{1,0:T(8,128)(2,1)S(1)}, bf16[2560,1024]{1,0:T(8,128)(2,1)}, u32[]{:S(2)}) copy-start(bf16[2560,1024]{1,0:T(8,128)(2,1)} %copy-done) | copy-start | bytes 15728644

commit v2 on v1

--- a/solution.py
+++ b/solution.py
@@ -124,9 +124,18 @@
     return lax.dot_general(a, b, (((1,), (1,)), ((), ())), preferred_element_type=jnp.float32)
 
 
-def request_kernel(plan, coords_ref, owner_ref, bin_ref, out_ref, x_ref):
+def request_kernel(plan, coords_in, owner_in, bin_in, out_ref, x_ref, coords_ref, owner_ref, bin_ref, sem):
     p = plan
     row_count = p.cells // LANES
+    copies = [
+        pltpu.make_async_copy(owner_in, owner_ref, sem.at[0]),
+        pltpu.make_async_copy(bin_in, bin_ref, sem.at[1]),
+        pltpu.make_async_copy(coords_in, coords_ref, sem.at[2]),
+    ]
+    for copy in copies:
+        copy.start()
+    for copy in copies:
+        copy.wait()
     half = iota((1, LANES), 1) // GROUP
     shard_ids = iota((p.table, LANES), 0)
     owners = owner_ref[...]
@@ -204,7 +213,18 @@
 
 
 def lookup_kernel(
-    plan, recv_ref, table_ref, out_ref, ints_ref, near_idx, far_idx, w_near, w_far, sem, *gathered
+    plan,
+    recv_ref,
+    table_ref,
+    out_ref,
+    ints_ref,
+    near_idx,
+    far_idx,
+    w_near,
+    w_far,
+    g_near,
+    g_far,
+    sem,
 ):
     p = plan
     ints_ref[0] = recv_ref[pl.ds(4, p.devices, stride=8), :].astype(jnp.int32)
@@ -219,8 +239,20 @@
     lane = iota((1, LANES), 1)
     spread = (iota((3 * K, LANES), 0) % K == iota((3 * K, LANES), 1) % K).astype(jnp.float32)
     spread = spread.astype(jnp.bfloat16)
-
-    def weigh(u, carry):
+    chunk_rows = LANES * p.cols
+    for copy in copies:
+        copy.wait()
+
+    def fetch(store, at, address):
+        if p.cols == 1:
+            store[pl.ds(at, 1), :] = table_ref[pl.ds(address, 1), :]
+        else:
+            store[pl.ds(at, p.cols, stride=8), :] = table_ref[pl.ds(address, p.cols, stride=8), :]
+
+    def first_of(chunk, slot):
+        return chunk * chunk_rows + (slot // 8) * (8 * p.cols) + slot % 8
+
+    def serve(u, carry):
         blocks = [
             recv_ref[pl.ds(pl.multiple_of((4 * u + i) * 8, 8), 8), :] for i in range(4)
         ]
@@ -241,65 +273,74 @@
         for i in range(4):
             src = 4 * u + i
             t, s = src // p.scal, src % p.scal
+            near_at, far_at = first_of(s, t * p.near), first_of(s, t * p.quad)
             for g in range(p.table):
+                for q in range(p.near):
+                    fetch(
+                        g_near,
+                        near_at + g * p.scal * chunk_rows + q,
+                        near_idx[src, g * p.near + q],
+                    )
                 start = (g * p.scal + s) * LANES + t * p.near
                 w_near[pl.ds(pl.multiple_of(start, p.near), p.near), :] = weights[
                     i * LANES + g * p.near : i * LANES + (g + 1) * p.near
                 ]
             for q in range(p.table // 4):
+                for j in range(p.quad):
+                    fetch(
+                        g_far,
+                        far_at + q * p.scal * chunk_rows + j,
+                        far_idx[src, q * p.quad + j],
+                    )
                 start = (q * p.scal + s) * LANES + t * p.quad
                 row = 4 * LANES + 32 * i + q * p.quad
                 w_far[pl.ds(pl.multiple_of(start, p.quad), p.quad), :] = weights[row : row + p.quad]
         return carry
 
-    lax.fori_loop(0, p.devices // 4, weigh, 0)
-    for copy in copies:
-        copy.wait()
-
-    depth = p.cols * LANES
-    choose = (iota((p.scalars, depth), 0) == iota((p.scalars, depth), 1) // K).astype(jnp.float32)
-    choose = jnp.concatenate([choose.astype(jnp.bfloat16)] * 2, axis=1)
-
-    def fetch(store, slot, address):
-        if p.cols == 1:
-            store[pl.ds(slot, 1), :] = table_ref[pl.ds(address, 1), :]
-        else:
-            store[pl.ds(slot, p.cols, stride=LANES), :] = table_ref[
-                pl.ds(address, p.cols, stride=8), :
+    lax.fori_loop(0, p.devices // 4, serve, 0)
+
+    step = min(2, p.cols)
+    depth = step * LANES
+    choices = []
+    for c in range(0, p.cols, step):
+        choose = iota((p.scalars, depth), 0) == (c * LANES + iota((p.scalars, depth), 1)) // K
+        choices.append(choose.astype(jnp.float32).astype(jnp.bfloat16))
+
+    def reduce(store, weight_ref, chunk):
+        weights = weight_ref[pl.ds(pl.multiple_of(chunk * LANES, LANES), 2 * LANES), :]
+        first = pl.multiple_of(chunk * chunk_rows, chunk_rows)
+        total = None
+        for c in range(0, p.cols, step):
+            high, low = [], []
+            for e in range(c, c + step):
+                tiles = [
+                    store[pl.ds(first + (b * p.cols + e) * 8, 8), :] for b in range(LANES // 4)
+                ]
+                two = pieces_of(jnp.concatenate(tiles, axis=0) * weights, 2)
+                high.append(two[0])
+                low.append(two[1])
+            for half in (high, low):
+                part = dot_rows(choices[c // step], jnp.concatenate(half, axis=1))
+                total = part if total is None else total + part
+        return total
+
+    def near_chunks(pair, carry):
+        both = reduce(g_near, w_near, 2 * pair)
+        for i in range(2):
+            out_ref[pl.ds((2 * pair + i) * p.rows, p.scalars), :] = both[
+                :, i * LANES : (i + 1) * LANES
             ]
-
-    def reduce(store, weights):
-        high, low = [], []
-        for c in range(p.cols):
-            product = store[c * LANES : (c + 1) * LANES, :] * weights
-            two = pieces_of(product, 2)
-            high.append(two[0])
-            low.append(two[1])
-        return dot_rows(choose, jnp.concatenate(high + low, axis=1))
-
-    def near_chunks(g, carry):
-        for s in range(p.scal):
-            for t in range(p.table):
-                for q in range(p.near):
-                    fetch(gathered[s], t * p.near + q, near_idx[t * p.scal + s, g * p.near + q])
-        for s in range(p.scal):
-            dest = g * p.scal + s
-            weights = w_near[pl.ds(pl.multiple_of(dest * LANES, LANES), LANES), :]
-            out_ref[pl.ds(dest * p.rows, p.scalars), :] = reduce(gathered[s], weights)
         return carry
 
-    lax.fori_loop(0, p.table, near_chunks, 0)
+    lax.fori_loop(0, p.devices // 2, near_chunks, 0)
     quad_of = (lane // p.far) % 4
 
-    def far_chunks(quad, carry):
-        for s in range(p.scal):
-            for t in range(p.table):
-                for q in range(p.quad):
-                    fetch(gathered[s], t * p.quad + q, far_idx[t * p.scal + s, quad * p.quad + q])
-        for s in range(p.scal):
-            chunk = quad * p.scal + s
-            weights = w_far[pl.ds(pl.multiple_of(chunk * LANES, LANES), LANES), :]
-            tile = reduce(gathered[s], weights)
+    def far_chunks(pair, carry):
+        both = reduce(g_far, w_far, 2 * pair)
+        for n in range(2):
+            chunk = 2 * pair + n
+            quad, s = chunk // p.scal, chunk % p.scal
+            tile = both[:, n * LANES : (n + 1) * LANES]
             for i in range(4):
                 message = jnp.zeros((p.few, LANES), jnp.float32)
                 for b in range(4):
@@ -311,7 +352,7 @@
                 out_ref[pl.ds(dest * p.rows + p.scalars, p.few), :] = message
         return carry
 
-    lax.fori_loop(0, p.table // 4, far_chunks, 0)
+    lax.fori_loop(0, p.devices // 8, far_chunks, 0)
 
 
 def slots_kernel(plan, me_ref, recv_ref, out_ref):
@@ -418,8 +459,14 @@
         request_kernel,
         p,
         jax.ShapeDtypeStruct((p.devices, 8, LANES), f32),
-        [VMEM] * 3,
-        [pltpu.VMEM((8, p.cells), f32)],
+        [pl.BlockSpec(memory_space=pl.ANY)] * 3,
+        [
+            pltpu.VMEM((8, p.cells), f32),
+            pltpu.VMEM(cell_coords.shape, f32),
+            pltpu.VMEM(owners.shape, i32),
+            pltpu.VMEM(bins.shape, i32),
+            pltpu.SemaphoreType.DMA((3,)),
+        ],
         32,
         1 << 20,
         "requests",
@@ -440,10 +487,11 @@
             pltpu.SMEM((p.devices, LANES), i32),
             pltpu.VMEM((p.devices * LANES, LANES), f32),
             pltpu.VMEM((p.devices * LANES // 4, LANES), f32),
+            pltpu.VMEM((p.devices * LANES * p.cols, LANES), f32),
+            pltpu.VMEM((p.devices * LANES * p.cols // 4, LANES), f32),
             pltpu.SemaphoreType.DMA((2,)),
-        ]
-        + [pltpu.VMEM((p.cols * LANES, LANES), f32) for _ in range(p.scal)],
-        48,
+        ],
+        8 + (5 * p.devices * (p.cols + 1)) // 64 + (depth * bin_count >> 18),
         1 << 24,
         "lookup",
     )(received, table)
@@ -457,7 +505,7 @@
         jax.ShapeDtypeStruct((p.table * 5 * LANES // 4, LG * p.nx), jnp.bfloat16),
         [SMEM, VMEM],
         [],
-        48,
+        8 + p.nx * p.table // 128,
         1 << 24,
         "slots",
     )(me, received)
@@ -470,7 +518,7 @@
         (out, out),
         [VMEM] * 3,
         [pltpu.VMEM((SCAL_ALL, p.table * 5 * LANES // 4), f32)],
-        48,
+        8 + p.nx * p.table // 64,
         1 << 24,
         "filter",
     )(answers, place, jnp.asarray(both_op.astype(np.float32)))

time: 59.6 us -> 58.3 us (0.978)
  Pallas kernels: 25.7 us -> 21 us
  local copies, waits for them, and re-layouts: 6.91 us -> 10.3 us
    pallas_call x1, Pallas kernels: 21.1 us -> 16.4 us  [on_device(): call(lookup_kernel, p, jax.ShapeDtypeStruct((p.devices * p.rows, LANES),...]
    unnamed x12 -> x14, local copies, waits for them, and re-layouts: 6.91 us -> 10.3 us
where the time goes in v2:
time: 58.3 us; the launch traced here: 57.9 us
  Pallas kernels  21 us (36%)
  blocking collectives  15.7 us (27%)
  local copies, waits for them, and re-layouts  10.3 us (18%)
  waiting for transfers between devices  7.47 us (13%)
  starting transfers between devices  2.61 us (4%)
  between operations  0.69 us (1%)
    pallas_call x1, Pallas kernels, on_device(): call(lookup_kernel, p, jax.ShapeDtypeStruct((p.devices * p.rows, LANES),...  16.4 us
    all_to_all x1, blocking collectives, exchange(): return lax.all_to_all(array, AXES, split_axis=0, concat_axis=0, tiled=True)  15.7 us
    unnamed x14, local copies, waits for them, and re-layouts  10.3 us
    all_to_all x1, waiting for transfers between devices, exchange(): return lax.all_to_all(array, AXES, split_axis=0, concat_axis=0, tiled=True)  7.47 us
    all_to_all x1, starting transfers between devices, exchange(): return lax.all_to_all(array, AXES, split_axis=0, concat_axis=0, tiled=True)  2.61 us
    pallas_call x1, Pallas kernels, on_device(): call(filter_kernel, p, (out, out), [VMEM] * 3, [pltpu.VMEM((SCAL_ALL, p.t...  2.05 us
    pallas_call x1, Pallas kernels, on_device(): call(slots_kernel, p, jax.ShapeDtypeStruct((p.table * 5 * LANES // 4, LG...  1.87 us
  transfers between devices with their start and end apart: 1, of which 1 were waited for; matrix products, arithmetic and copies ran while one was open for 0% of the time, Pallas kernels for 3%

profile of v2, /device:TPU:0, one launch (start us, length us, event | category | flops | bytes accessed | tf_op | source)
XLA Modules:
  0.0 57.9 jit_solution(11657976095202570306)
XLA Ops:
  0.6 0.0 copy-start.3
  0.6 0.0 copy-start.4
  0.7 0.7 %copy-done.4 = f32[4,1024]{1,0:T(4,128)S(1)} copy-done((f32[4,1024]{1,0:T(4,128)S(1)}, f32[4,1024]{1,0:T(4,128)}, u32[]{:S(2)}) %copy-start.4) | copy-done | bytes 16408
  1.4 0.0 copy-start.5
  1.4 0.7 %copy-done.5 = s32[1024,1]{0,1:T(1,128)S(1)} copy-done((s32[1024,1]{0,1:T(1,128)S(1)}, s32[1024,1]{0,1:T(1,128)}, u32[]{:S(2)}) %copy-start.5) | copy-done | bytes 4120
  2.1 0.0 copy-start.6
  2.1 0.7 %copy-done.6 = s32[1024]{0:T(1024)S(1)} copy-done((s32[1024]{0:T(1024)S(1)}, s32[1024]{0:T(1024)}, u32[]{:S(2)}) %copy-start.6) | copy-done | bytes 4120
  2.8 0.7 %requests.1 = f32[32,8,128]{2,1,0:T(8,128)S(1)} custom-call(f32[4,1024]{1,0:T(4,128)S(1)} %copy-done.4, s32[8,128]{1,0:T(8,128)S(1)} %bitcast.16, s32[8,128]{1,0:T(8,128)S(1)} %bitcast.17), custom_call_target="tpu_custom_call" | custom-call | flops 1048576 | bytes 4096 | tf_op jit(solution)/shard_map/requests/pallas_call | solution.py:458
  3.5 15.7 %all_to_all.10 = f32[32,8,128]{2,1,0:T(8,128)S(1)} all-to-all(f32[32,8,128]{2,1,0:T(8,128)S(1)} %requests.1), channel_id=1, replica_groups=mesh['table'=16,'scal'=2] {'table','scal'}, dimensions={0} | all-to-all | bytes 262144 | tf_op jit(solution)/shard_map/all_to_all | solution.py:449
  19.2 0.0 copy-start.2
  19.2 3.4 %copy-done.2 = f32[4096,512]{1,0:T(8,128)S(1)} copy-done((f32[4096,512]{1,0:T(8,128)S(1)}, f32[4096,512]{1,0:T(8,128)}, u32[]{:S(2)}) %copy-start.2) | copy-done | bytes 8388632
  22.6 16.4 %lookup.1 = f32[640,128]{1,0:T(8,128)} custom-call(f32[256,128]{1,0:T(8,128)S(1)} %bitcast.14, f32[16384,128]{1,0:T(8,128)S(1)} %bitcast.12), custom_call_target="tpu_custom_call" | custom-call | flops 16777216 | bytes 65536 | tf_op jit(solution)/shard_map/lookup/pallas_call | solution.py:479
  39.0 2.6 %all-to-all-start.1 = ((f32[32,1,2560]{2,1,0:T(1,128)}), f32[32,1,2560]{2,1,0:T(1,128)S(1)}, u32[]{:S(2)}, u32[]{:S(2)}) async-start(f32[32,1,2560]{2,1,0:T(1,128)} %bitcast.6), calls=%async_computation.1 | async-start | bytes 655360 | tf_op jit(solution)/shard_map/all_to_all | solution.py:449
  41.6 0.1 pad_add_fusion.me_ref
  41.7 1.9 %slots.1.place_ref = bf16[2560,1024]{1,0:T(8,128)(2,1)S(1)} custom-call(s32[2]{0:T(128)S(1)} %pad_add_fusion.me_ref, f32[256,128]{1,0:T(8,128)S(1)} %bitcast.15), custom_call_target="tpu_custom_call" | custom-call | flops 16777216 | bytes 65536 | tf_op jit(solution)/shard_map/slots/pallas_call | solution.py:502
  43.6 0.0 copy-start
  43.6 2.3 %copy-done = bf16[2560,1024]{1,0:T(8,128)(2,1)} copy-done((bf16[2560,1024]{1,0:T(8,128)(2,1)}, bf16[2560,1024]{1,0:T(8,128)(2,1)S(1)}, u32[]{:S(2)}) %copy-start) | copy-done | bytes 5242904
  45.9 7.5 %all-to-all-done.1 = f32[32,1,2560]{2,1,0:T(1,128)S(1)} async-done(((f32[32,1,2560]{2,1,0:T(1,128)}), f32[32,1,2560]{2,1,0:T(1,128)S(1)}, u32[]{:S(2)}, u32[]{:S(2)}) %all-to-all-start.1) | async-done | bytes 327712 | tf_op jit(solution)/shard_map/all_to_all | solution.py:449
  53.3 0.0 copy-done.3
  53.3 0.0 copy-start.1
  53.3 2.5 %copy-done.1 = bf16[2560,1024]{1,0:T(8,128)(2,1)S(1)} copy-done((bf16[2560,1024]{1,0:T(8,128)(2,1)S(1)}, bf16[2560,1024]{1,0:T(8,128)(2,1)}, u32[]{:S(2)}) %copy-start.1) | copy-done | bytes 5242904
  55.8 2.1 %filter.1 = (f32[32,8,128]{2,1,0:T(8,128)}, f32[32,8,128]{2,1,0:T(8,128)}) custom-call(f32[640,128]{1,0:T(8,128)S(1)} %bitcast.13, bf16[2560,1024]{1,0:T(8,128)(2,1)S(1)} %copy-done.1, f32[128,256]{1,0:T(8,128)S(1)} %copy-done.3), custom_call_target="tpu_custom_call" | custom-call | flops 16777216 | bytes 65536 | tf_op jit(solution)/shard_map/filter/pallas_call | solution.py:515
Async XLA Ops:
  0.6 52.7 %copy-start.3 = (f32[128,256]{1,0:T(8,128)S(1)}, f32[128,256]{1,0:T(8,128)}, u32[]{:S(2)}) copy-start(f32[128,256]{1,0:T(8,128)} %constant.10.clone.op_ref) | copy-start | bytes 393220
  0.6 0.8 %copy-start.4 = (f32[4,1024]{1,0:T(4,128)S(1)}, f32[4,1024]{1,0:T(4,128)}, u32[]{:S(2)}) copy-start(f32[4,1024]{1,0:T(4,128)} %coords_in.1) | copy-start | bytes 49156
  1.4 0.7 %copy-start.5 = (s32[1024,1]{0,1:T(1,128)S(1)}, s32[1024,1]{0,1:T(1,128)}, u32[]{:S(2)}) copy-start(s32[1024,1]{0,1:T(1,128)} %param.7) | copy-start | bytes 12292
  2.1 0.7 %copy-start.6 = (s32[1024]{0:T(1024)S(1)}, s32[1024]{0:T(1024)}, u32[]{:S(2)}) copy-start(s32[1024]{0:T(1024)} %param.8) | copy-start | bytes 12292
  19.2 3.4 %copy-start.2 = (f32[4096,512]{1,0:T(8,128)S(1)}, f32[4096,512]{1,0:T(8,128)}, u32[]{:S(2)}) copy-start(f32[4096,512]{1,0:T(8,128)} %param.6) | copy-start | bytes 25165828
  39.0 14.3 %all-to-all-start.1 = ((f32[32,1,2560]{2,1,0:T(1,128)}), f32[32,1,2560]{2,1,0:T(1,128)S(1)}, u32[]{:S(2)}, u32[]{:S(2)}) async-start(f32[32,1,2560]{2,1,0:T(1,128)} %bitcast.6), calls=%async_computation.1 | async-start | bytes 655360 | tf_op jit(solution)/shard_map/all_to_all | solution.py:449
  43.6 2.3 %copy-start = (bf16[2560,1024]{1,0:T(8,128)(2,1)}, bf16[2560,1024]{1,0:T(8,128)(2,1)S(1)}, u32[]{:S(2)}) copy-start(bf16[2560,1024]{1,0:T(8,128)(2,1)S(1)} %slots.1.place_ref) | copy-start | bytes 15728644
  53.3 2.5 %copy-start.1 = (bf16[2560,1024]{1,0:T(8,128)(2,1)S(1)}, bf16[2560,1024]{1,0:T(8,128)(2,1)}, u32[]{:S(2)}) copy-start(bf16[2560,1024]{1,0:T(8,128)(2,1)} %copy-done) | copy-start | bytes 15728644

commit v3 on v1

--- a/solution.py
+++ b/solution.py
@@ -15,6 +15,8 @@
 GROUP = BX * LG
 LANES = 128
 AXES = ("table", "scal")
+BATCH = 4
+PARTS = 4
 
 strength = 0.499
 
@@ -104,6 +106,7 @@
         self.few = self.scalars // 4
         self.rows = self.scalars + self.few
         self.nx = BX * table
+        self.chunks = self.devices + self.devices // 4
 
 
 def iota(shape, dim):
@@ -124,9 +127,18 @@
     return lax.dot_general(a, b, (((1,), (1,)), ((), ())), preferred_element_type=jnp.float32)
 
 
-def request_kernel(plan, coords_ref, owner_ref, bin_ref, out_ref, x_ref):
+def request_kernel(plan, coords_in, owner_in, bin_in, out_ref, x_ref, coords_ref, owner_ref, bin_ref, sem):
     p = plan
     row_count = p.cells // LANES
+    copies = [
+        pltpu.make_async_copy(owner_in, owner_ref, sem.at[0]),
+        pltpu.make_async_copy(bin_in, bin_ref, sem.at[1]),
+        pltpu.make_async_copy(coords_in, coords_ref, sem.at[2]),
+    ]
+    for copy in copies:
+        copy.start()
+    for copy in copies:
+        copy.wait()
     half = iota((1, LANES), 1) // GROUP
     shard_ids = iota((p.table, LANES), 0)
     owners = owner_ref[...]
@@ -203,179 +215,235 @@
     return product * cubic
 
 
+def swap_blocks(x, count, width):
+    row, block = iota(x.shape, 0), iota(x.shape, 1) // width
+    bit = 1
+    while bit < count:
+        up = pltpu.roll(pltpu.roll(x, x.shape[0] - bit, 0), bit * width, 1)
+        down = pltpu.roll(pltpu.roll(x, bit, 0), LANES - bit * width, 1)
+        low_row, low_block = (row & bit) == 0, (block & bit) == 0
+        x = jnp.where(low_row == low_block, x, jnp.where(low_row, up, down))
+        bit *= 2
+    return x
+
+
 def lookup_kernel(
-    plan, recv_ref, table_ref, out_ref, ints_ref, near_idx, far_idx, w_near, w_far, sem, *gathered
+    plan,
+    recv_ref,
+    table_in,
+    out_ref,
+    table_ref,
+    ints_ref,
+    idx_ref,
+    field_ref,
+    tile_ref,
+    sem,
+    *stores,
 ):
     p = plan
-    ints_ref[0] = recv_ref[pl.ds(4, p.devices, stride=8), :].astype(jnp.int32)
-    ints_ref[1] = recv_ref[pl.ds(6, p.devices, stride=8), :].astype(jnp.int32)
-    copies = [
-        pltpu.make_async_copy(ints_ref.at[0], near_idx, sem.at[0]),
-        pltpu.make_async_copy(ints_ref.at[1], far_idx, sem.at[1]),
+    quads = p.table // 4
+    part = table_ref.shape[0] // PARTS
+    loads = [
+        pltpu.make_async_copy(
+            table_in.at[pl.ds(i * part, part)], table_ref.at[pl.ds(i * part, part)], sem.at[1 + i]
+        )
+        for i in range(PARTS)
     ]
-    for copy in copies:
-        copy.start()
-
-    lane = iota((1, LANES), 1)
-    spread = (iota((3 * K, LANES), 0) % K == iota((3 * K, LANES), 1) % K).astype(jnp.float32)
-    spread = spread.astype(jnp.bfloat16)
-
-    def weigh(u, carry):
-        blocks = [
-            recv_ref[pl.ds(pl.multiple_of((4 * u + i) * 8, 8), 8), :] for i in range(4)
+    for load in loads[: PARTS // 2]:
+        load.start()
+
+    def received(r):
+        rows = [recv_ref[pl.ds(s * 8 + r, p.table, stride=8 * p.scal), :] for s in range(p.scal)]
+        return jnp.concatenate(rows, axis=0)
+
+    addresses = jnp.concatenate([received(4), received(6)], axis=0)
+    addresses = swap_blocks(addresses, p.table, p.near).astype(jnp.int32)
+    ints_ref[0 : p.devices, :] = addresses[: p.devices]
+    for s in range(p.scal):
+        first = p.devices + s * p.table
+        to = p.devices + s * quads
+        ints_ref[to : to + quads, :] = addresses[first : first + quads]
+    copy = pltpu.make_async_copy(ints_ref, idx_ref, sem.at[0])
+    copy.start()
+    for load in loads[PARTS // 2 :]:
+        load.start()
+    fields = jnp.concatenate([received(f) for f in (0, 1, 2, 3, 5)], axis=0)
+    fields = swap_blocks(fields, p.table, p.near)
+    for f in range(4):
+        field_ref[f * p.chunks : f * p.chunks + p.devices, :] = fields[
+            f * p.devices : (f + 1) * p.devices
         ]
-        parts = [spline_rows([block[f : f + 1, :] for f in range(4)]) for block in blocks]
-        far = []
-        for f in range(4):
-            row = jnp.zeros((1, LANES), jnp.float32)
-            for i in range(4):
-                turned = pltpu.roll(blocks[i][5:6, :], (32 * (i - f)) % LANES, 1)
-                row = jnp.where(lane // 32 == i, turned, row)
-            far.append(row)
-        parts.append(spline_rows(far))
-        rows = jnp.concatenate(parts, axis=1)
-        rows = jnp.concatenate(pieces_of(rows, 3), axis=0)
-        weights = lax.dot_general(
-            rows, spread, (((0,), (0,)), ((), ())), preferred_element_type=jnp.float32
-        )
-        for i in range(4):
-            src = 4 * u + i
-            t, s = src // p.scal, src % p.scal
-            for g in range(p.table):
-                start = (g * p.scal + s) * LANES + t * p.near
-                w_near[pl.ds(pl.multiple_of(start, p.near), p.near), :] = weights[
-                    i * LANES + g * p.near : i * LANES + (g + 1) * p.near
+        for s in range(p.scal):
+            first = 4 * p.devices + s * p.table + f * quads
+            to = f * p.chunks + p.devices + s * quads
+            field_ref[to : to + quads, :] = fields[first : first + quads]
+    copy.wait()
+
+    part_rows = p.scalars * 8
+    shape = (p.scalars, 2 * part_rows)
+    choose = (iota(shape, 0) == (iota(shape, 1) % part_rows) // 8).astype(jnp.float32)
+    choose = choose.astype(jnp.bfloat16)
+
+    def fetch(store, chunk, part):
+        step = LANES // p.cols
+        for slot in range(part * step, (part + 1) * step):
+            address = idx_ref[chunk, slot]
+            at = (slot // 8) * (8 * p.cols) + slot % 8
+            if p.cols == 1:
+                store[pl.ds(at, 1), :] = table_ref[pl.ds(address, 1), :]
+            else:
+                store[pl.ds(at, p.cols, stride=8), :] = table_ref[
+                    pl.ds(address, p.cols, stride=8), :
                 ]
-            for q in range(p.table // 4):
-                start = (q * p.scal + s) * LANES + t * p.quad
-                row = 4 * LANES + 32 * i + q * p.quad
-                w_far[pl.ds(pl.multiple_of(start, p.quad), p.quad), :] = weights[row : row + p.quad]
+
+    def reduce(store, chunk, ahead):
+        weights = spline_rows([field_ref[pl.ds(f * p.chunks + chunk, 1), :] for f in range(4)])
+        parts = []
+        for c in range(p.cols):
+            tiles = [store[(b * p.cols + c) * 8 : (b * p.cols + c + 1) * 8, :] for b in range(16)]
+            turned = jnp.concatenate(tiles, axis=0).T
+            for m in range(4):
+                product = turned[m * K : (m + 1) * K] * weights
+                parts.append((product[0:8] + product[8:16]) + (product[16:24] + product[24:32]))
+            ahead(c)
+        parts = jnp.concatenate(pieces_of(jnp.concatenate(parts, axis=0), 2), axis=0)
+        tile = jnp.dot(choose, parts, preferred_element_type=jnp.float32)
+        tile_ref[pl.ds(pl.multiple_of(chunk * p.scalars, p.scalars), p.scalars), :] = tile
+
+    for load in loads:
+        load.wait()
+    for n in range(BATCH):
+        for c in range(p.cols):
+            fetch(stores[n], n, c)
+
+    def two_batches(i, carry):
+        for half in range(2):
+            now = (2 * i + half) * BATCH
+            later = jnp.minimum(now + BATCH, p.chunks - BATCH)
+            for n in range(BATCH):
+                ahead = functools.partial(fetch, stores[(1 - half) * BATCH + n], later + n)
+                reduce(stores[half * BATCH + n], now + n, ahead)
         return carry
 
-    lax.fori_loop(0, p.devices // 4, weigh, 0)
-    for copy in copies:
-        copy.wait()
-
-    depth = p.cols * LANES
-    choose = (iota((p.scalars, depth), 0) == iota((p.scalars, depth), 1) // K).astype(jnp.float32)
-    choose = jnp.concatenate([choose.astype(jnp.bfloat16)] * 2, axis=1)
-
-    def fetch(store, slot, address):
-        if p.cols == 1:
-            store[pl.ds(slot, 1), :] = table_ref[pl.ds(address, 1), :]
-        else:
-            store[pl.ds(slot, p.cols, stride=LANES), :] = table_ref[
-                pl.ds(address, p.cols, stride=8), :
+    lax.fori_loop(0, p.chunks // (2 * BATCH), two_batches, 0)
+
+    for g in range(p.table):
+        for s in range(p.scal):
+            dest, chunk = g * p.scal + s, s * p.table + g
+            out_ref[dest * p.rows : dest * p.rows + p.scalars, :] = tile_ref[
+                chunk * p.scalars : (chunk + 1) * p.scalars, :
             ]
-
-    def reduce(store, weights):
-        high, low = [], []
-        for c in range(p.cols):
-            product = store[c * LANES : (c + 1) * LANES, :] * weights
-            two = pieces_of(product, 2)
-            high.append(two[0])
-            low.append(two[1])
-        return dot_rows(choose, jnp.concatenate(high + low, axis=1))
-
-    def near_chunks(g, carry):
+    quad_of = (iota((1, LANES), 1) // p.far) % 4
+    for quad in range(quads):
         for s in range(p.scal):
-            for t in range(p.table):
-                for q in range(p.near):
-                    fetch(gathered[s], t * p.near + q, near_idx[t * p.scal + s, g * p.near + q])
-        for s in range(p.scal):
-            dest = g * p.scal + s
-            weights = w_near[pl.ds(pl.multiple_of(dest * LANES, LANES), LANES), :]
-            out_ref[pl.ds(dest * p.rows, p.scalars), :] = reduce(gathered[s], weights)
-        return carry
-
-    lax.fori_loop(0, p.table, near_chunks, 0)
-    quad_of = (lane // p.far) % 4
-
-    def far_chunks(quad, carry):
-        for s in range(p.scal):
-            for t in range(p.table):
-                for q in range(p.quad):
-                    fetch(gathered[s], t * p.quad + q, far_idx[t * p.scal + s, quad * p.quad + q])
-        for s in range(p.scal):
-            chunk = quad * p.scal + s
-            weights = w_far[pl.ds(pl.multiple_of(chunk * LANES, LANES), LANES), :]
-            tile = reduce(gathered[s], weights)
+            first = (p.devices + s * quads + quad) * p.scalars
+            tile = tile_ref[first : first + p.scalars, :]
+            turned = [pltpu.roll(tile, (d * p.far) % LANES, 1) if d else tile for d in range(4)]
+            wrapped = [
+                pltpu.roll(tile, (-d * p.far) % LANES, 1) if d else tile for d in range(4)
+            ]
             for i in range(4):
                 message = jnp.zeros((p.few, LANES), jnp.float32)
                 for b in range(4):
-                    turned = pltpu.roll(
-                        tile[b * p.few : (b + 1) * p.few], ((b - i) * p.far) % LANES, 1
+                    moved = turned[b - i] if b >= i else wrapped[i - b]
+                    message = jnp.where(
+                        quad_of == b, moved[b * p.few : (b + 1) * p.few], message
                     )
-                    message = jnp.where(quad_of == b, turned, message)
-                dest = (quad * 4 + i) * p.scal + s
-                out_ref[pl.ds(dest * p.rows + p.scalars, p.few), :] = message
-        return carry
-
-    lax.fori_loop(0, p.table // 4, far_chunks, 0)
+                start = ((quad * 4 + i) * p.scal + s) * p.rows + p.scalars
+                out_ref[start : start + p.few, :] = message
+
+
+def lookup_scratch(plan, table_shape):
+    p = plan
+    return [
+        pltpu.VMEM(table_shape, jnp.float32),
+        pltpu.VMEM((p.chunks, LANES), jnp.int32),
+        pltpu.SMEM((p.chunks, LANES), jnp.int32),
+        pltpu.VMEM((4 * p.chunks, LANES), jnp.float32),
+        pltpu.VMEM((p.chunks * p.scalars, LANES), jnp.float32),
+        pltpu.SemaphoreType.DMA((1 + PARTS,)),
+    ] + [pltpu.VMEM((p.cols * LANES, LANES), jnp.float32) for _ in range(2 * BATCH)]
 
 
 def slots_kernel(plan, me_ref, recv_ref, out_ref):
     p = plan
     table_at, scal_at = me_ref[0], me_ref[1]
-    width = LG * p.nx
-    codes = recv_ref[pl.ds(scal_at * 8 + 7, p.table, stride=8 * p.scal), :]
-    cell = iota((LANES, width), 1)
-    inside = (cell // p.nx) * BX + cell % BX + GROUP * (table_at % 2)
-    move = (iota((LANES, width), 0) == inside).astype(jnp.float32).astype(jnp.bfloat16)
-    moved = jnp.dot(codes.astype(jnp.bfloat16), move, preferred_element_type=jnp.float32)
-    x_block = (iota((p.table, width), 1) % p.nx) // BX
-    moved = jnp.where(iota((p.table, width), 0) == x_block, moved, 0.0)
-    code = jnp.sum(moved, axis=0, keepdims=True).astype(jnp.int32)
-    shard, slot = code // p.code, code % p.code
-    t = (iota((1, width), 1) % p.nx) // BX
-    near = jnp.where(slot < p.near, shard * LANES + t * p.near + slot, -1)
-    far = jnp.where(
-        slot >= p.near,
-        (shard // 4 + p.table) * LANES + t * p.quad + (shard % 4) * p.far + slot - p.near,
-        -1,
-    )
-    chosen = jnp.where(slot < p.near, near, far)
+    half_x = p.nx // 2
+    width = LG * half_x
+    codes = recv_ref[pl.ds(scal_at * 8 + 7, p.table, stride=8 * p.scal), :].astype(jnp.bfloat16)
     step = 2 * LANES
-    rows = iota((step, width), 0)
-
-    def fill(i, carry):
-        start = pl.multiple_of(i * step, step)
-        hit = rows == chosen - start
-        out_ref[pl.ds(start, step), :] = jnp.where(hit, 1.0, 0.0).astype(jnp.bfloat16)
-        return carry
-
-    lax.fori_loop(0, out_ref.shape[0] // step, fill, 0)
-
-
-def filter_kernel(plan, recv_ref, place_ref, op_ref, filtered_ref, gradient_ref, left_ref):
+    for h in range(2):
+        x = iota((1, width), 1) % half_x + h * half_x
+        inside = (iota((1, width), 1) // half_x) * BX + x % BX + GROUP * (table_at % 2)
+        move = (iota((LANES, width), 0) == inside).astype(jnp.float32).astype(jnp.bfloat16)
+        moved = jnp.dot(codes, move, preferred_element_type=jnp.float32)
+        t = x // BX
+        moved = jnp.where(iota((p.table, width), 0) == t, moved, 0.0)
+        code = jnp.sum(moved, axis=0, keepdims=True).astype(jnp.int32)
+        shard, slot = code // p.code, code % p.code
+        t = t - h * (p.table // 2)
+        near = (shard // 2) * LANES + (shard % 2) * GROUP + t * p.near + slot
+        quad = shard // 4
+        far = (p.table // 2 + quad // 2) * LANES + (quad % 2) * GROUP
+        far = far + t * p.quad + (shard % 4) * p.far + slot - p.near
+        chosen = jnp.where(slot < p.near, near, far)
+        rows = iota((step, width), 0)
+
+        def fill(i, carry):
+            start = pl.multiple_of(i * step, step)
+            hit = rows == chosen - start
+            out_ref[h, pl.ds(start, step), :] = jnp.where(hit, 1.0, 0.0).astype(jnp.bfloat16)
+            return carry
+
+        lax.fori_loop(0, out_ref.shape[1] // step, fill, 0)
+
+
+def filter_kernel(plan, recv_ref, place_ref, op_ref, filtered_ref, gradient_ref, *left_refs):
     p = plan
     lane = iota((1, LANES), 1)
+    low = lane < GROUP
     quad_of = (lane // p.far) % 4
-    for o in range(p.table):
+
+    def halves(first, second, rows, col):
+        turned = [pltpu.roll(tile, GROUP, 1) for tile in (first, second)]
+        left_refs[0][rows, col : col + LANES] = jnp.where(low, first, turned[1])
+        left_refs[1][rows, col : col + LANES] = jnp.where(low, turned[0], second)
+
+    for o in range(0, p.table, 2):
         for sc in range(p.scal):
-            start = (o * p.scal + sc) * p.rows
-            left_ref[sc * p.scalars : (sc + 1) * p.scalars, o * LANES : (o + 1) * LANES] = recv_ref[
-                start : start + p.scalars, :
-            ]
-    for quad in range(p.table // 4):
+            tiles = []
+            for i in range(2):
+                start = ((o + i) * p.scal + sc) * p.rows
+                tiles.append(recv_ref[start : start + p.scalars, :])
+            halves(*tiles, slice(sc * p.scalars, (sc + 1) * p.scalars), o // 2 * LANES)
+    for quad in range(0, p.table // 4, 2):
         for sc in range(p.scal):
-            messages = []
-            for i in range(4):
-                start = ((quad * 4 + i) * p.scal + sc) * p.rows + p.scalars
-                messages.append(recv_ref[start : start + p.few, :])
             for b in range(4):
-                part = jnp.zeros((p.few, LANES), jnp.float32)
-                for i in range(4):
-                    turned = pltpu.roll(messages[i], ((i - b) * p.far) % LANES, 1)
-                    part = jnp.where(quad_of == i, turned, part)
+                parts = []
+                for n in range(2):
+                    part = jnp.zeros((p.few, LANES), jnp.float32)
+                    for i in range(4):
+                        start = (((quad + n) * 4 + i) * p.scal + sc) * p.rows + p.scalars
+                        turned = recv_ref[start : start + p.few, :]
+                        turned = pltpu.roll(turned, ((i - b) * p.far) % LANES, 1)
+                        part = jnp.where(quad_of == i, turned, part)
+                    parts.append(part)
                 row = sc * p.scalars + b * p.few
-                col = (p.table + quad) * LANES
-                left_ref[row : row + p.few, col : col + LANES] = part
-    left = jnp.concatenate(pieces_of(left_ref[...], 3), axis=0)
-    values = jnp.dot(left, place_ref[...], preferred_element_type=jnp.float32)
-    values = values[0:SCAL_ALL] + values[SCAL_ALL : 2 * SCAL_ALL] + values[2 * SCAL_ALL :]
+                halves(*parts, slice(row, row + p.few), (p.table + quad) // 2 * LANES)
+    sides = []
+    for h in range(2):
+        left = jnp.concatenate(pieces_of(left_refs[h][...], 3), axis=0)
+        values = jnp.dot(left, place_ref[h], preferred_element_type=jnp.float32)
+        sides.append(
+            values[0:SCAL_ALL] + values[SCAL_ALL : 2 * SCAL_ALL] + values[2 * SCAL_ALL :]
+        )
+    half_x = p.nx // 2
     lines = jnp.concatenate(
-        [values[:, r * p.nx : (r + 1) * p.nx] for r in range(LG)], axis=0
+        [
+            jnp.concatenate([side[:, r * half_x : (r + 1) * half_x] for side in sides], axis=1)
+            for r in range(LG)
+        ],
+        axis=0,
     )
     both = jnp.dot(
         lines, op_ref[...], precision=lax.Precision.HIGHEST, preferred_element_type=jnp.float32
@@ -388,6 +456,7 @@
 
 VMEM = pl.BlockSpec(memory_space=pltpu.VMEM)
 SMEM = pl.BlockSpec(memory_space=pltpu.SMEM)
+HBM = pl.BlockSpec(memory_space=pltpu.HBM)
 
 
 def call(kernel, plan, out_shape, in_specs, scratch, limit, cost, name):
@@ -418,9 +487,15 @@
         request_kernel,
         p,
         jax.ShapeDtypeStruct((p.devices, 8, LANES), f32),
-        [VMEM] * 3,
-        [pltpu.VMEM((8, p.cells), f32)],
-        32,
+        [HBM] * 3,
+        [
+            pltpu.VMEM((8, p.cells), f32),
+            pltpu.VMEM(cell_coords.shape, f32),
+            pltpu.VMEM(owners.shape, i32),
+            pltpu.VMEM(bins.shape, i32),
+            pltpu.SemaphoreType.DMA((3,)),
+        ],
+        60,
         1 << 20,
         "requests",
     )(cell_coords, owners, bins)
@@ -433,17 +508,9 @@
         lookup_kernel,
         p,
         jax.ShapeDtypeStruct((p.devices * p.rows, LANES), f32),
-        [VMEM] * 2,
-        [
-            pltpu.VMEM((2, p.devices, LANES), i32),
-            pltpu.SMEM((p.devices, LANES), i32),
-            pltpu.SMEM((p.devices, LANES), i32),
-            pltpu.VMEM((p.devices * LANES, LANES), f32),
-            pltpu.VMEM((p.devices * LANES // 4, LANES), f32),
-            pltpu.SemaphoreType.DMA((2,)),
-        ]
-        + [pltpu.VMEM((p.cols * LANES, LANES), f32) for _ in range(p.scal)],
-        48,
+        [VMEM, HBM],
+        lookup_scratch(p, table.shape),
+        50,
         1 << 24,
         "lookup",
     )(received, table)
@@ -454,10 +521,10 @@
     place = call(
         slots_kernel,
         p,
-        jax.ShapeDtypeStruct((p.table * 5 * LANES // 4, LG * p.nx), jnp.bfloat16),
+        jax.ShapeDtypeStruct((2, p.table * 5 * LANES // 8, LG * p.nx // 2), jnp.bfloat16),
         [SMEM, VMEM],
         [],
-        48,
+        8 + p.nx * p.table // 128,
         1 << 24,
         "slots",
     )(me, received)
@@ -469,8 +536,8 @@
         p,
         (out, out),
         [VMEM] * 3,
-        [pltpu.VMEM((SCAL_ALL, p.table * 5 * LANES // 4), f32)],
-        48,
+        [pltpu.VMEM((SCAL_ALL, p.table * 5 * LANES // 8), f32)] * 2,
+        8 + p.nx * p.table // 64,
         1 << 24,
         "filter",
     )(answers, place, jnp.asarray(both_op.astype(np.float32)))

time: 59.6 us -> 47.4 us (0.80)
  Pallas kernels: 25.7 us -> 17.6 us
  local copies, waits for them, and re-layouts: 6.91 us -> 0.01 us
  waiting for transfers between devices: 7.46 us -> 10.1 us
    pallas_call x1, Pallas kernels: 21.1 us -> 12.1 us  [on_device(): call(lookup_kernel, p, jax.ShapeDtypeStruct((p.devices * p.rows, LANES),...]
    unnamed x12 -> x2, local copies, waits for them, and re-layouts: 6.91 us -> 0.01 us
    all_to_all x1, waiting for transfers between devices: 7.46 us -> 10.1 us  [exchange(): return lax.all_to_all(array, AXES, split_axis=0, concat_axis=0, tiled=True)]
    pallas_call x1, Pallas kernels: 0.68 us -> 2.15 us  [on_device(): call(request_kernel, p, jax.ShapeDtypeStruct((p.devices, 8, LANES), f32),...]
where the time goes in v3:
time: 47.4 us; the launch traced here: 47 us
  Pallas kernels  17.6 us (37%)
  blocking collectives  15.9 us (34%)
  waiting for transfers between devices  10.1 us (21%)
  starting transfers between devices  2.61 us (6%)
  between operations  0.67 us (1%)
    all_to_all x1, blocking collectives, exchange(): return lax.all_to_all(array, AXES, split_axis=0, concat_axis=0, tiled=True)  15.9 us
    pallas_call x1, Pallas kernels, on_device(): call(lookup_kernel, p, jax.ShapeDtypeStruct((p.devices * p.rows, LANES),...  12.1 us
    all_to_all x1, waiting for transfers between devices, exchange(): return lax.all_to_all(array, AXES, split_axis=0, concat_axis=0, tiled=True)  10.1 us
    all_to_all x1, starting transfers between devices, exchange(): return lax.all_to_all(array, AXES, split_axis=0, concat_axis=0, tiled=True)  2.61 us
    pallas_call x1, Pallas kernels, on_device(): call(request_kernel, p, jax.ShapeDtypeStruct((p.devices, 8, LANES), f32),...  2.15 us
    pallas_call x1, Pallas kernels, on_device(): call(filter_kernel, p, (out, out), [VMEM] * 3, [pltpu.VMEM((SCAL_ALL, p.t...  1.79 us
    pallas_call x1, Pallas kernels, on_device(): call(slots_kernel, p, jax.ShapeDtypeStruct((2, p.table * 5 * LANES // 8,...  1.53 us
  transfers between devices with their start and end apart: 1, of which 1 were waited for; matrix products, arithmetic and copies ran while one was open for 0% of the time, Pallas kernels for 3%

profile of v3, /device:TPU:0, one launch (start us, length us, event | category | flops | bytes accessed | tf_op | source)
XLA Modules:
  0.0 47.0 jit_solution(8365738995711202515)
XLA Ops:
  0.6 0.0 copy-start
  0.6 2.1 %requests.1 = f32[32,8,128]{2,1,0:T(8,128)} custom-call(f32[4,1024]{1,0:T(4,128)} %coords_in.1, s32[8,128]{1,0:T(8,128)} %bitcast.16, s32[8,128]{1,0:T(8,128)} %bitcast.17), custom_call_target="tpu_custom_call" | custom-call | flops 1048576 | bytes 4096 | tf_op jit(solution)/shard_map/requests/pallas_call | solution.py:486
  2.8 15.9 %all_to_all.10 = f32[32,8,128]{2,1,0:T(8,128)S(1)} all-to-all(f32[32,8,128]{2,1,0:T(8,128)} %requests.1), channel_id=1, replica_groups=mesh['table'=16,'scal'=2] {'table','scal'}, dimensions={0} | all-to-all | bytes 262144 | tf_op jit(solution)/shard_map/all_to_all | solution.py:477
  18.7 12.1 %lookup.1 = f32[640,128]{1,0:T(8,128)} custom-call(f32[256,128]{1,0:T(8,128)S(1)} %bitcast.13, f32[16384,128]{1,0:T(8,128)} %bitcast.15), custom_call_target="tpu_custom_call" | custom-call | flops 16777216 | bytes 65536 | tf_op jit(solution)/shard_map/lookup/pallas_call | solution.py:507
  30.9 2.6 %all-to-all-start.1 = ((f32[32,1,2560]{2,1,0:T(1,128)}), f32[32,1,2560]{2,1,0:T(1,128)S(1)}, u32[]{:S(2)}, u32[]{:S(2)}) async-start(f32[32,1,2560]{2,1,0:T(1,128)} %bitcast.6), calls=%async_computation.1 | async-start | bytes 655360 | tf_op jit(solution)/shard_map/all_to_all | solution.py:477
  33.5 0.1 pad_add_fusion.me_ref
  33.6 1.5 %slots.1.place_ref = bf16[2,1280,512]{2,1,0:T(8,128)(2,1)S(1)} custom-call(s32[2]{0:T(128)S(1)} %pad_add_fusion.me_ref, f32[256,128]{1,0:T(8,128)S(1)} %bitcast.14), custom_call_target="tpu_custom_call" | custom-call | flops 16777216 | bytes 65536 | tf_op jit(solution)/shard_map/slots/pallas_call | solution.py:521
  35.1 10.1 %all-to-all-done.1 = f32[32,1,2560]{2,1,0:T(1,128)S(1)} async-done(((f32[32,1,2560]{2,1,0:T(1,128)}), f32[32,1,2560]{2,1,0:T(1,128)S(1)}, u32[]{:S(2)}, u32[]{:S(2)}) %all-to-all-start.1) | async-done | bytes 327712 | tf_op jit(solution)/shard_map/all_to_all | solution.py:477
  45.2 0.0 copy-done
  45.2 1.8 %filter.1 = (f32[32,8,128]{2,1,0:T(8,128)}, f32[32,8,128]{2,1,0:T(8,128)}) custom-call(f32[640,128]{1,0:T(8,128)S(1)} %bitcast.12, bf16[2,1280,512]{2,1,0:T(8,128)(2,1)S(1)} %slots.1.place_ref, f32[128,256]{1,0:T(8,128)S(1)} %copy-done), custom_call_target="tpu_custom_call" | custom-call | flops 16777216 | bytes 65536 | tf_op jit(solution)/shard_map/filter/pallas_call | solution.py:534
Async XLA Ops:
  0.6 44.6 %copy-start = (f32[128,256]{1,0:T(8,128)S(1)}, f32[128,256]{1,0:T(8,128)}, u32[]{:S(2)}) copy-start(f32[128,256]{1,0:T(8,128)} %constant.10.clone.op_ref) | copy-start | bytes 393220
  30.9 14.3 %all-to-all-start.1 = ((f32[32,1,2560]{2,1,0:T(1,128)}), f32[32,1,2560]{2,1,0:T(1,128)S(1)}, u32[]{:S(2)}, u32[]{:S(2)}) async-start(f32[32,1,2560]{2,1,0:T(1,128)} %bitcast.6), calls=%async_computation.1 | async-start | bytes 655360 | tf_op jit(solution)/shard_map/all_to_all | solution.py:477

commit v4 on v3

--- a/solution.py
+++ b/solution.py
@@ -16,7 +16,6 @@
 LANES = 128
 AXES = ("table", "scal")
 BATCH = 4
-PARTS = 4
 
 strength = 0.499
 
@@ -230,6 +229,7 @@
 def lookup_kernel(
     plan,
     recv_ref,
+    early_ref,
     table_in,
     out_ref,
     table_ref,
@@ -242,15 +242,20 @@
 ):
     p = plan
     quads = p.table // 4
-    part = table_ref.shape[0] // PARTS
+    early = early_ref.shape[0]
+    late = table_ref.shape[0] - early
     loads = [
         pltpu.make_async_copy(
-            table_in.at[pl.ds(i * part, part)], table_ref.at[pl.ds(i * part, part)], sem.at[1 + i]
-        )
-        for i in range(PARTS)
+            table_in.at[pl.ds(early, late // 2)], table_ref.at[pl.ds(early, late // 2)], sem.at[1]
+        ),
+        pltpu.make_async_copy(
+            table_in.at[pl.ds(early + late // 2, late // 2)],
+            table_ref.at[pl.ds(early + late // 2, late // 2)],
+            sem.at[2],
+        ),
+        pltpu.make_async_copy(early_ref, table_ref.at[pl.ds(0, early)], sem.at[3]),
     ]
-    for load in loads[: PARTS // 2]:
-        load.start()
+    loads[0].start()
 
     def received(r):
         rows = [recv_ref[pl.ds(s * 8 + r, p.table, stride=8 * p.scal), :] for s in range(p.scal)]
@@ -265,7 +270,7 @@
         ints_ref[to : to + quads, :] = addresses[first : first + quads]
     copy = pltpu.make_async_copy(ints_ref, idx_ref, sem.at[0])
     copy.start()
-    for load in loads[PARTS // 2 :]:
+    for load in loads[1:]:
         load.start()
     fields = jnp.concatenate([received(f) for f in (0, 1, 2, 3, 5)], axis=0)
     fields = swap_blocks(fields, p.table, p.near)
@@ -279,20 +284,14 @@
             field_ref[to : to + quads, :] = fields[first : first + quads]
     copy.wait()
 
-    part_rows = p.scalars * 8
-    shape = (p.scalars, 2 * part_rows)
-    choose = (iota(shape, 0) == (iota(shape, 1) % part_rows) // 8).astype(jnp.float32)
-    choose = choose.astype(jnp.bfloat16)
-
     def fetch(store, chunk, part):
         step = LANES // p.cols
         for slot in range(part * step, (part + 1) * step):
             address = idx_ref[chunk, slot]
-            at = (slot // 8) * (8 * p.cols) + slot % 8
             if p.cols == 1:
-                store[pl.ds(at, 1), :] = table_ref[pl.ds(address, 1), :]
+                store[slot : slot + 1, :] = table_ref[pl.ds(address, 1), :]
             else:
-                store[pl.ds(at, p.cols, stride=8), :] = table_ref[
+                store[slot * p.cols : (slot + 1) * p.cols, :] = table_ref[
                     pl.ds(address, p.cols, stride=8), :
                 ]
 
@@ -300,14 +299,13 @@
         weights = spline_rows([field_ref[pl.ds(f * p.chunks + chunk, 1), :] for f in range(4)])
         parts = []
         for c in range(p.cols):
-            tiles = [store[(b * p.cols + c) * 8 : (b * p.cols + c + 1) * 8, :] for b in range(16)]
-            turned = jnp.concatenate(tiles, axis=0).T
+            rows = pl.ds(c, LANES, stride=p.cols) if p.cols > 1 else pl.ds(0, LANES)
+            turned = store[rows, :].T
             for m in range(4):
                 product = turned[m * K : (m + 1) * K] * weights
                 parts.append((product[0:8] + product[8:16]) + (product[16:24] + product[24:32]))
             ahead(c)
-        parts = jnp.concatenate(pieces_of(jnp.concatenate(parts, axis=0), 2), axis=0)
-        tile = jnp.dot(choose, parts, preferred_element_type=jnp.float32)
+        tile = jnp.sum(jnp.concatenate(parts, axis=0).reshape(p.scalars, 8, LANES), axis=1)
         tile_ref[pl.ds(pl.multiple_of(chunk * p.scalars, p.scalars), p.scalars), :] = tile
 
     for load in loads:
@@ -361,7 +359,7 @@
         pltpu.SMEM((p.chunks, LANES), jnp.int32),
         pltpu.VMEM((4 * p.chunks, LANES), jnp.float32),
         pltpu.VMEM((p.chunks * p.scalars, LANES), jnp.float32),
-        pltpu.SemaphoreType.DMA((1 + PARTS,)),
+        pltpu.SemaphoreType.DMA((4,)),
     ] + [pltpu.VMEM((p.cols * LANES, LANES), jnp.float32) for _ in range(2 * BATCH)]
 
 
@@ -504,16 +502,17 @@
     bin_count, depth = flamelet_table.shape
     table = flamelet_table.reshape(bin_count // 8, 8, p.cols, LANES).transpose(0, 2, 1, 3)
     table = table.reshape(bin_count * p.cols, LANES)
+    early = table[: bin_count * p.cols * 11 // 32]
     replies = call(
         lookup_kernel,
         p,
         jax.ShapeDtypeStruct((p.devices * p.rows, LANES), f32),
-        [VMEM, HBM],
+        [VMEM, VMEM, HBM],
         lookup_scratch(p, table.shape),
         50,
         1 << 24,
         "lookup",
-    )(received, table)
+    )(received, early, table)
     answers = exchange(replies.reshape(p.devices, 1, p.rows * LANES))
     answers = answers.reshape(p.devices * p.rows, LANES)
 

time: 47.4 us -> 45.2 us (0.954)
  blocking collectives: 15.9 us -> 0 us
  starting transfers between devices: 2.61 us -> 10 us
  waiting for transfers between devices: 10.1 us -> 16.6 us
  Pallas kernels: 17.6 us -> 15.3 us
  local copies, waits for them, and re-layouts: 0.01 us -> 2.1 us
    all_to_all x1 -> x0, blocking collectives: 15.9 us -> none  [exchange(): return lax.all_to_all(array, AXES, split_axis=0, concat_axis=0, tiled=True)]
    all_to_all x1 -> x2, starting transfers between devices: 2.61 us -> 10 us  [exchange(): return lax.all_to_all(array, AXES, split_axis=0, concat_axis=0, tiled=True)]
    all_to_all x1 -> x2, waiting for transfers between devices: 10.1 us -> 16.6 us  [exchange(): return lax.all_to_all(array, AXES, split_axis=0, concat_axis=0, tiled=True)]
    pallas_call x1, Pallas kernels: 12.1 us -> 9.82 us  [on_device(): call(lookup_kernel, p, jax.ShapeDtypeStruct((p.devices * p.rows, LANES),...]
    slice x0 -> x1, local copies, waits for them, and re-layouts: none -> 2.09 us  [on_device(): early = table[:bin_count * p.cols * 11 // 32]]
  transfers between devices with their start and end apart: 1 -> 2, of which waited for: 1 -> 2; matrix products, arithmetic and copies ran while one was open for 0% -> 5% of each run, Pallas kernels for 3% -> 3%
where the time goes in v4:
time: 45.2 us; the launch traced here: 44.8 us
  waiting for transfers between devices  16.6 us (37%)
  Pallas kernels  15.3 us (34%)
  starting transfers between devices  10 us (22%)
  local copies, waits for them, and re-layouts  2.1 us (5%)
  between operations  0.69 us (2%)
    all_to_all x2, waiting for transfers between devices, exchange(): return lax.all_to_all(array, AXES, split_axis=0, concat_axis=0, tiled=True)  16.6 us
    all_to_all x2, starting transfers between devices, exchange(): return lax.all_to_all(array, AXES, split_axis=0, concat_axis=0, tiled=True)  10 us
    pallas_call x1, Pallas kernels, on_device(): call(lookup_kernel, p, jax.ShapeDtypeStruct((p.devices * p.rows, LANES),...  9.82 us
    pallas_call x1, Pallas kernels, on_device(): call(request_kernel, p, jax.ShapeDtypeStruct((p.devices, 8, LANES), f32),...  2.11 us
    slice x1, local copies, waits for them, and re-layouts, on_device(): early = table[:bin_count * p.cols * 11 // 32]  2.09 us
    pallas_call x1, Pallas kernels, on_device(): call(filter_kernel, p, (out, out), [VMEM] * 3, [pltpu.VMEM((SCAL_ALL, p.t...  1.79 us
    pallas_call x1, Pallas kernels, on_device(): call(slots_kernel, p, jax.ShapeDtypeStruct((2, p.table * 5 * LANES // 8,...  1.53 us
  transfers between devices with their start and end apart: 2, of which 2 were waited for; matrix products, arithmetic and copies ran while one was open for 5% of the time, Pallas kernels for 3%

profile of v4, /device:TPU:0, one launch (start us, length us, event | category | flops | bytes accessed | tf_op | source)
XLA Modules:
  0.0 44.8 jit_solution(7222608340686166914)
XLA Ops:
  0.6 2.1 %requests.1 = f32[32,8,128]{2,1,0:T(8,128)} custom-call(f32[4,1024]{1,0:T(4,128)} %coords_in.1, s32[8,128]{1,0:T(8,128)} %bitcast.19, s32[8,128]{1,0:T(8,128)} %bitcast.20), custom_call_target="tpu_custom_call" | custom-call | flops 1048576 | bytes 4096 | tf_op jit(solution)/shard_map/requests/pallas_call | solution.py:484
  2.8 7.3 %all-to-all-start = ((f32[32,8,128]{2,1,0:T(8,128)}), f32[32,8,128]{2,1,0:T(8,128)S(1)}, u32[]{:S(2)}, u32[]{:S(2)}) async-start(f32[32,8,128]{2,1,0:T(8,128)} %requests.1), calls=%async_computation | async-start | bytes 262144 | tf_op jit(solution)/shard_map/all_to_all | solution.py:475
  10.1 2.1 %slice.8 = f32[176,4,8,128]{3,2,1,0:T(8,128)S(1)} slice(f32[512,4,8,128]{3,2,1,0:T(8,128)} %bitcast.17), slice={[0:176], [0:4], [0:8], [0:128]} | slice | bytes 5767168 | tf_op jit(solution)/shard_map/slice | solution.py:505
  12.2 6.5 %all-to-all-done = f32[32,8,128]{2,1,0:T(8,128)S(1)} async-done(((f32[32,8,128]{2,1,0:T(8,128)}), f32[32,8,128]{2,1,0:T(8,128)S(1)}, u32[]{:S(2)}, u32[]{:S(2)}) %all-to-all-start) | async-done | bytes 131104 | tf_op jit(solution)/shard_map/all_to_all | solution.py:475
  18.7 9.8 %lookup.1 = f32[640,128]{1,0:T(8,128)} custom-call(f32[256,128]{1,0:T(8,128)S(1)} %bitcast.15, f32[5632,128]{1,0:T(8,128)S(1)} %bitcast.13, f32[16384,128]{1,0:T(8,128)} %bitcast.18), custom_call_target="tpu_custom_call" | custom-call | flops 16777216 | bytes 65536 | tf_op jit(solution)/shard_map/lookup/pallas_call | solution.py:506
  28.5 0.0 copy-start
  28.5 2.7 %all-to-all-start.1 = ((f32[32,1,2560]{2,1,0:T(1,128)}), f32[32,1,2560]{2,1,0:T(1,128)S(1)}, u32[]{:S(2)}, u32[]{:S(2)}) async-start(f32[32,1,2560]{2,1,0:T(1,128)} %bitcast.8), calls=%async_computation.1 | async-start | bytes 655360 | tf_op jit(solution)/shard_map/all_to_all | solution.py:475
  31.3 0.1 pad_add_fusion.me_ref
  31.4 1.5 %slots.1.place_ref = bf16[2,1280,512]{2,1,0:T(8,128)(2,1)S(1)} custom-call(s32[2]{0:T(128)S(1)} %pad_add_fusion.me_ref, f32[256,128]{1,0:T(8,128)S(1)} %bitcast.16), custom_call_target="tpu_custom_call" | custom-call | flops 16777216 | bytes 65536 | tf_op jit(solution)/shard_map/slots/pallas_call | solution.py:520
  32.9 10.1 %all-to-all-done.1 = f32[32,1,2560]{2,1,0:T(1,128)S(1)} async-done(((f32[32,1,2560]{2,1,0:T(1,128)}), f32[32,1,2560]{2,1,0:T(1,128)S(1)}, u32[]{:S(2)}, u32[]{:S(2)}) %all-to-all-start.1) | async-done | bytes 327712 | tf_op jit(solution)/shard_map/all_to_all | solution.py:475
  43.0 0.0 copy-done
  43.0 1.8 %filter.1 = (f32[32,8,128]{2,1,0:T(8,128)}, f32[32,8,128]{2,1,0:T(8,128)}) custom-call(f32[640,128]{1,0:T(8,128)S(1)} %bitcast.14, bf16[2,1280,512]{2,1,0:T(8,128)(2,1)S(1)} %slots.1.place_ref, f32[128,256]{1,0:T(8,128)S(1)} %copy-done), custom_call_target="tpu_custom_call" | custom-call | flops 16777216 | bytes 65536 | tf_op jit(solution)/shard_map/filter/pallas_call | solution.py:533
Async XLA Ops:
  2.8 15.9 %all-to-all-start = ((f32[32,8,128]{2,1,0:T(8,128)}), f32[32,8,128]{2,1,0:T(8,128)S(1)}, u32[]{:S(2)}, u32[]{:S(2)}) async-start(f32[32,8,128]{2,1,0:T(8,128)} %requests.1), calls=%async_computation | async-start | bytes 262144 | tf_op jit(solution)/shard_map/all_to_all | solution.py:475
  28.5 14.5 %copy-start = (f32[128,256]{1,0:T(8,128)S(1)}, f32[128,256]{1,0:T(8,128)}, u32[]{:S(2)}) copy-start(f32[128,256]{1,0:T(8,128)} %constant.10.clone.op_ref) | copy-start | bytes 393220
  28.5 14.5 %all-to-all-start.1 = ((f32[32,1,2560]{2,1,0:T(1,128)}), f32[32,1,2560]{2,1,0:T(1,128)S(1)}, u32[]{:S(2)}, u32[]{:S(2)}) async-start(f32[32,1,2560]{2,1,0:T(1,128)} %bitcast.8), calls=%async_computation.1 | async-start | bytes 655360 | tf_op jit(solution)/shard_map/all_to_all | solution.py:475

commit v5 on v4

--- a/solution.py
+++ b/solution.py
@@ -106,6 +106,7 @@
         self.rows = self.scalars + self.few
         self.nx = BX * table
         self.chunks = self.devices + self.devices // 4
+        self.padded = -(-self.chunks // LANES) * LANES
 
 
 def iota(shape, dim):
@@ -172,8 +173,11 @@
             ).astype(jnp.bfloat16)
         )
         fields = x_ref[:, i * LANES : (i + 1) * LANES]
-        chosen = jnp.where(hits[i][:, None, :], fields[None], 0.0).reshape(p.table * 8, LANES)
-        left.append(jnp.concatenate(pieces_of(chosen, 3), axis=0))
+        chosen = []
+        for piece in pieces_of(fields, 3):
+            piece = jnp.where(hits[i][:, None, :], piece.astype(jnp.float32)[None], 0.0)
+            chosen.append(piece.reshape(p.table * 8, LANES).astype(jnp.bfloat16))
+        left.append(jnp.concatenate(chosen, axis=0))
     placed = dot_rows(jnp.concatenate(left, axis=1), jnp.concatenate(right, axis=1))
     total = p.table * 8
     placed = placed[0:total] + placed[total : 2 * total] + placed[2 * total :]
@@ -234,13 +238,13 @@
     out_ref,
     table_ref,
     ints_ref,
-    idx_ref,
     field_ref,
     tile_ref,
     sem,
-    *stores,
+    *rest,
 ):
     p = plan
+    idx_refs, stores = rest[:16], rest[16:]
     quads = p.table // 4
     early = early_ref.shape[0]
     late = table_ref.shape[0] - early
@@ -262,14 +266,23 @@
         return jnp.concatenate(rows, axis=0)
 
     addresses = jnp.concatenate([received(4), received(6)], axis=0)
-    addresses = swap_blocks(addresses, p.table, p.near).astype(jnp.int32)
-    ints_ref[0 : p.devices, :] = addresses[: p.devices]
+    addresses = swap_blocks(addresses, p.table, p.near)
+    order = [addresses[: p.devices]]
     for s in range(p.scal):
         first = p.devices + s * p.table
-        to = p.devices + s * quads
-        ints_ref[to : to + quads, :] = addresses[first : first + quads]
-    copy = pltpu.make_async_copy(ints_ref, idx_ref, sem.at[0])
-    copy.start()
+        order.append(addresses[first : first + quads])
+    blank = p.padded - p.chunks
+    order.append(jnp.zeros((blank, LANES), jnp.float32))
+    order = jnp.concatenate(order, axis=0)
+    for first in range(0, p.padded, LANES):
+        turned = order[first : first + LANES].T
+        ints_ref[:, first : first + LANES] = turned.astype(jnp.int32)
+    copies = [
+        pltpu.make_async_copy(ints_ref.at[pl.ds(8 * i, 8)], idx_refs[i], sem.at[0])
+        for i in range(16)
+    ]
+    for copy in copies:
+        copy.start()
     for load in loads[1:]:
         load.start()
     fields = jnp.concatenate([received(f) for f in (0, 1, 2, 3, 5)], axis=0)
@@ -282,12 +295,13 @@
             first = 4 * p.devices + s * p.table + f * quads
             to = f * p.chunks + p.devices + s * quads
             field_ref[to : to + quads, :] = fields[first : first + quads]
-    copy.wait()
+    for copy in copies:
+        copy.wait()
 
     def fetch(store, chunk, part):
         step = LANES // p.cols
         for slot in range(part * step, (part + 1) * step):
-            address = idx_ref[chunk, slot]
+            address = idx_refs[slot // 8][slot % 8, chunk]
             if p.cols == 1:
                 store[slot : slot + 1, :] = table_ref[pl.ds(address, 1), :]
             else:
@@ -295,7 +309,7 @@
                     pl.ds(address, p.cols, stride=8), :
                 ]
 
-    def reduce(store, chunk, ahead):
+    def reduce(store, chunk, ahead=None):
         weights = spline_rows([field_ref[pl.ds(f * p.chunks + chunk, 1), :] for f in range(4)])
         parts = []
         for c in range(p.cols):
@@ -304,7 +318,8 @@
             for m in range(4):
                 product = turned[m * K : (m + 1) * K] * weights
                 parts.append((product[0:8] + product[8:16]) + (product[16:24] + product[24:32]))
-            ahead(c)
+            if ahead is not None:
+                ahead(c)
         tile = jnp.sum(jnp.concatenate(parts, axis=0).reshape(p.scalars, 8, LANES), axis=1)
         tile_ref[pl.ds(pl.multiple_of(chunk * p.scalars, p.scalars), p.scalars), :] = tile
 
@@ -314,16 +329,22 @@
         for c in range(p.cols):
             fetch(stores[n], n, c)
 
+    def batch(now, half, more):
+        for n in range(BATCH):
+            ahead = None
+            if more:
+                store = stores[(1 - half) * BATCH + n]
+                ahead = functools.partial(fetch, store, now + BATCH + n)
+            reduce(stores[half * BATCH + n], now + n, ahead)
+
     def two_batches(i, carry):
-        for half in range(2):
-            now = (2 * i + half) * BATCH
-            later = jnp.minimum(now + BATCH, p.chunks - BATCH)
-            for n in range(BATCH):
-                ahead = functools.partial(fetch, stores[(1 - half) * BATCH + n], later + n)
-                reduce(stores[half * BATCH + n], now + n, ahead)
+        batch(2 * i * BATCH, 0, True)
+        batch((2 * i + 1) * BATCH, 1, True)
         return carry
 
-    lax.fori_loop(0, p.chunks // (2 * BATCH), two_batches, 0)
+    lax.fori_loop(0, p.chunks // (2 * BATCH) - 1, two_batches, 0)
+    batch(p.chunks - 2 * BATCH, 0, True)
+    batch(p.chunks - BATCH, 1, False)
 
     for g in range(p.table):
         for s in range(p.scal):
@@ -355,12 +376,11 @@
     p = plan
     return [
         pltpu.VMEM(table_shape, jnp.float32),
-        pltpu.VMEM((p.chunks, LANES), jnp.int32),
-        pltpu.SMEM((p.chunks, LANES), jnp.int32),
+        pltpu.VMEM((LANES, p.padded), jnp.int32),
         pltpu.VMEM((4 * p.chunks, LANES), jnp.float32),
         pltpu.VMEM((p.chunks * p.scalars, LANES), jnp.float32),
         pltpu.SemaphoreType.DMA((4,)),
-    ] + [pltpu.VMEM((p.cols * LANES, LANES), jnp.float32) for _ in range(2 * BATCH)]
+    ] + [pltpu.SMEM((8, p.padded), jnp.int32)] * 16 + [pltpu.VMEM((p.cols * LANES, LANES), jnp.float32) for _ in range(2 * BATCH)]
 
 
 def slots_kernel(plan, me_ref, recv_ref, out_ref):
@@ -448,8 +468,11 @@
     )
     for r in range(LG):
         rows = slice(r * SCAL_ALL, (r + 1) * SCAL_ALL)
-        filtered_ref[:, r, :] = both[rows, : p.nx]
-        gradient_ref[:, r, :] = both[rows, p.nx :]
+        for part in range(p.nx // LANES):
+            at = pl.ds(part * SCAL_ALL * LG + r, SCAL_ALL, stride=LG)
+            first = part * LANES
+            filtered_ref[at, :] = both[rows, first : first + LANES]
+            gradient_ref[at, :] = both[rows, p.nx + first : p.nx + first + LANES]
 
 
 VMEM = pl.BlockSpec(memory_space=pltpu.VMEM)
@@ -529,8 +552,8 @@
     )(me, received)
     filter_op = filter_table(p.nx).T
     both_op = np.concatenate([filter_op, filter_op @ derivative_table(p.nx).T], axis=1)
-    out = jax.ShapeDtypeStruct((SCAL_ALL, LG, p.nx), f32)
-    return call(
+    out = jax.ShapeDtypeStruct((p.nx // LANES * SCAL_ALL * LG, LANES), f32)
+    outs = call(
         filter_kernel,
         p,
         (out, out),
@@ -540,6 +563,8 @@
         1 << 24,
         "filter",
     )(answers, place, jnp.asarray(both_op.astype(np.float32)))
+    outs = [out.reshape(p.nx // LANES, SCAL_ALL, LG, LANES).transpose(1, 2, 0, 3) for out in outs]
+    return tuple(out.reshape(SCAL_ALL, LG, p.nx) for out in outs)
 
 
 def solution(mesh):

time: 45.2 us -> 44.2 us (0.978)
  Pallas kernels: 15.3 us -> 14.2 us
    pallas_call x1, Pallas kernels: 9.82 us -> 8.91 us  [on_device(): call(lookup_kernel, p, jax.ShapeDtypeStruct((p.devices * p.rows, LANES),...]
where the time goes in v5:
time: 44.2 us; the launch traced here: 43.7 us
  waiting for transfers between devices  16.6 us (38%)
  Pallas kernels  14.2 us (32%)
  starting transfers between devices  10 us (23%)
  local copies, waits for them, and re-layouts  2.1 us (5%)
  between operations  0.69 us (2%)
    all_to_all x2, waiting for transfers between devices, exchange(): return lax.all_to_all(array, AXES, split_axis=0, concat_axis=0, tiled=True)  16.6 us
    all_to_all x2, starting transfers between devices, exchange(): return lax.all_to_all(array, AXES, split_axis=0, concat_axis=0, tiled=True)  10 us
    pallas_call x1, Pallas kernels, on_device(): call(lookup_kernel, p, jax.ShapeDtypeStruct((p.devices * p.rows, LANES),...  8.91 us
    slice x1, local copies, waits for them, and re-layouts, on_device(): early = table[:bin_count * p.cols * 11 // 32]  2.09 us
    pallas_call x1, Pallas kernels, on_device(): call(request_kernel, p, jax.ShapeDtypeStruct((p.devices, 8, LANES), f32),...  2.05 us
    pallas_call x1, Pallas kernels, on_device(): call(filter_kernel, p, (out, out), [VMEM] * 3, [pltpu.VMEM((SCAL_ALL, p.t...  1.71 us
    pallas_call x1, Pallas kernels, on_device(): call(slots_kernel, p, jax.ShapeDtypeStruct((2, p.table * 5 * LANES // 8,...  1.53 us
  transfers between devices with their start and end apart: 2, of which 2 were waited for; matrix products, arithmetic and copies ran while one was open for 5% of the time, Pallas kernels for 3%

profile of v5, /device:TPU:0, one launch (start us, length us, event | category | flops | bytes accessed | tf_op | source)
XLA Modules:
  0.0 43.7 jit_solution(18099098577722865177)
XLA Ops:
  0.6 2.1 %requests.1 = f32[32,8,128]{2,1,0:T(8,128)} custom-call(f32[4,1024]{1,0:T(4,128)} %coords_in.1, s32[8,128]{1,0:T(8,128)} %bitcast.21, s32[8,128]{1,0:T(8,128)} %bitcast.22), custom_call_target="tpu_custom_call" | custom-call | flops 1048576 | bytes 4096 | tf_op jit(solution)/shard_map/requests/pallas_call | solution.py:507
  2.7 7.3 %all-to-all-start = ((f32[32,8,128]{2,1,0:T(8,128)}), f32[32,8,128]{2,1,0:T(8,128)S(1)}, u32[]{:S(2)}, u32[]{:S(2)}) async-start(f32[32,8,128]{2,1,0:T(8,128)} %requests.1), calls=%async_computation | async-start | bytes 262144 | tf_op jit(solution)/shard_map/all_to_all | solution.py:498
  10.0 2.1 %slice.8 = f32[176,4,8,128]{3,2,1,0:T(8,128)S(1)} slice(f32[512,4,8,128]{3,2,1,0:T(8,128)} %bitcast.19), slice={[0:176], [0:4], [0:8], [0:128]} | slice | bytes 5767168 | tf_op jit(solution)/shard_map/slice | solution.py:528
  12.1 6.5 %all-to-all-done = f32[32,8,128]{2,1,0:T(8,128)S(1)} async-done(((f32[32,8,128]{2,1,0:T(8,128)}), f32[32,8,128]{2,1,0:T(8,128)S(1)}, u32[]{:S(2)}, u32[]{:S(2)}) %all-to-all-start) | async-done | bytes 131104 | tf_op jit(solution)/shard_map/all_to_all | solution.py:498
  18.6 8.9 %lookup.1 = f32[640,128]{1,0:T(8,128)} custom-call(f32[256,128]{1,0:T(8,128)S(1)} %bitcast.17, f32[5632,128]{1,0:T(8,128)S(1)} %bitcast.15, f32[16384,128]{1,0:T(8,128)} %bitcast.20), custom_call_target="tpu_custom_call" | custom-call | flops 16777216 | bytes 65536 | tf_op jit(solution)/shard_map/lookup/pallas_call | solution.py:529
  27.5 0.0 copy-start
  27.6 2.7 %all-to-all-start.1 = ((f32[32,1,2560]{2,1,0:T(1,128)}), f32[32,1,2560]{2,1,0:T(1,128)S(1)}, u32[]{:S(2)}, u32[]{:S(2)}) async-start(f32[32,1,2560]{2,1,0:T(1,128)} %bitcast.8), calls=%async_computation.1 | async-start | bytes 655360 | tf_op jit(solution)/shard_map/all_to_all | solution.py:498
  30.3 0.1 pad_add_fusion.me_ref
  30.4 1.5 %slots.1.place_ref = bf16[2,1280,512]{2,1,0:T(8,128)(2,1)S(1)} custom-call(s32[2]{0:T(128)S(1)} %pad_add_fusion.me_ref, f32[256,128]{1,0:T(8,128)S(1)} %bitcast.18), custom_call_target="tpu_custom_call" | custom-call | flops 16777216 | bytes 65536 | tf_op jit(solution)/shard_map/slots/pallas_call | solution.py:543
  31.9 10.1 %all-to-all-done.1 = f32[32,1,2560]{2,1,0:T(1,128)S(1)} async-done(((f32[32,1,2560]{2,1,0:T(1,128)}), f32[32,1,2560]{2,1,0:T(1,128)S(1)}, u32[]{:S(2)}, u32[]{:S(2)}) %all-to-all-start.1) | async-done | bytes 327712 | tf_op jit(solution)/shard_map/all_to_all | solution.py:498
  42.0 0.0 copy-done
  42.0 1.7 %filter.1 = (f32[256,128]{1,0:T(8,128)}, f32[256,128]{1,0:T(8,128)}) custom-call(f32[640,128]{1,0:T(8,128)S(1)} %bitcast.16, bf16[2,1280,512]{2,1,0:T(8,128)(2,1)S(1)} %slots.1.place_ref, f32[128,256]{1,0:T(8,128)S(1)} %copy-done), custom_call_target="tpu_custom_call" | custom-call | flops 16777216 | bytes 65536 | tf_op jit(solution)/shard_map/filter/pallas_call | solution.py:556
Async XLA Ops:
  2.7 15.9 %all-to-all-start = ((f32[32,8,128]{2,1,0:T(8,128)}), f32[32,8,128]{2,1,0:T(8,128)S(1)}, u32[]{:S(2)}, u32[]{:S(2)}) async-start(f32[32,8,128]{2,1,0:T(8,128)} %requests.1), calls=%async_computation | async-start | bytes 262144 | tf_op jit(solution)/shard_map/all_to_all | solution.py:498
  27.5 14.5 %copy-start = (f32[128,256]{1,0:T(8,128)S(1)}, f32[128,256]{1,0:T(8,128)}, u32[]{:S(2)}) copy-start(f32[128,256]{1,0:T(8,128)} %constant.10.clone.op_ref) | copy-start | bytes 393220
  27.6 14.5 %all-to-all-start.1 = ((f32[32,1,2560]{2,1,0:T(1,128)}), f32[32,1,2560]{2,1,0:T(1,128)S(1)}, u32[]{:S(2)}, u32[]{:S(2)}) async-start(f32[32,1,2560]{2,1,0:T(1,128)} %bitcast.8), calls=%async_computation.1 | async-start | bytes 655360 | tf_op jit(solution)/shard_map/all_to_all | solution.py:498

commit v6 on v5

--- a/solution.py
+++ b/solution.py
@@ -127,7 +127,20 @@
     return lax.dot_general(a, b, (((1,), (1,)), ((), ())), preferred_element_type=jnp.float32)
 
 
-def request_kernel(plan, coords_in, owner_in, bin_in, out_ref, x_ref, coords_ref, owner_ref, bin_ref, sem):
+def request_kernel(
+    plan,
+    coords_in,
+    owner_in,
+    bin_in,
+    table_in,
+    out_ref,
+    early_ref,
+    x_ref,
+    coords_ref,
+    owner_ref,
+    bin_ref,
+    sem,
+):
     p = plan
     row_count = p.cells // LANES
     copies = [
@@ -135,7 +148,10 @@
         pltpu.make_async_copy(bin_in, bin_ref, sem.at[1]),
         pltpu.make_async_copy(coords_in, coords_ref, sem.at[2]),
     ]
-    for copy in copies:
+    early = pltpu.make_async_copy(
+        table_in.at[pl.ds(0, early_ref.shape[0])], early_ref, sem.at[3]
+    )
+    for copy in copies + [early]:
         copy.start()
     for copy in copies:
         copy.wait()
@@ -194,6 +210,7 @@
         )
         for sc in range(p.scal):
             out_ref[o * p.scal + sc] = message
+    early.wait()
 
 
 def spline_rows(f):
@@ -230,12 +247,57 @@
     return x
 
 
+def fill_slots(plan, me_ref, recv_ref, out_ref):
+    p = plan
+    table_at, scal_at = me_ref[0], me_ref[1]
+    part_x = p.nx // 4
+    width = LG * part_x
+    codes = recv_ref[pl.ds(scal_at * 8 + 7, p.table, stride=8 * p.scal), :].astype(jnp.bfloat16)
+    step = LANES
+    for h in range(4):
+        x = iota((1, width), 1) % part_x + h * part_x
+        inside = (iota((1, width), 1) // part_x) * BX + x % BX + GROUP * (table_at % 2)
+        move = (iota((LANES, width), 0) == inside).astype(jnp.float32).astype(jnp.bfloat16)
+        moved = jnp.dot(codes, move, preferred_element_type=jnp.float32)
+        t = x // BX
+        moved = jnp.where(iota((p.table, width), 0) == t, moved, 0.0)
+        code = jnp.sum(moved, axis=0, keepdims=True).astype(jnp.int32)
+        shard, slot = code // p.code, code % p.code
+        t = t - h * (p.table // 4)
+        near = (shard // 4) * LANES + (shard % 4) * 32 + t * p.near + slot
+        quad = shard // 4
+        far = (p.table // 4 + quad // 4) * LANES + (quad % 4) * 32
+        far = far + t * p.quad + (shard % 4) * p.far + slot - p.near
+        chosen = jnp.where(slot < p.near, near, far)
+        rows = iota((step, width), 0)
+        for start in range(0, out_ref.shape[1], step):
+            hit = rows == chosen - start
+            out_ref[h, start : start + step, :] = jnp.where(hit, 1.0, 0.0).astype(jnp.bfloat16)
+
+
+def swap_four(tiles):
+    block = iota((1, LANES), 1) // 32
+    for bit in (2, 1):
+        low = (block & bit) == 0
+        turned = [pltpu.roll(tile, 32 * bit, 1) for tile in tiles]
+        back = [pltpu.roll(tile, LANES - 32 * bit, 1) for tile in tiles] if bit == 1 else turned
+        out = list(tiles)
+        for i in range(4):
+            if not i & bit:
+                out[i] = jnp.where(low, tiles[i], turned[i + bit])
+                out[i + bit] = jnp.where(low, back[i], tiles[i + bit])
+        tiles = out
+    return tiles
+
+
 def lookup_kernel(
     plan,
+    me_ref,
     recv_ref,
     early_ref,
     table_in,
     out_ref,
+    place_ref,
     table_ref,
     ints_ref,
     field_ref,
@@ -295,6 +357,7 @@
             first = 4 * p.devices + s * p.table + f * quads
             to = f * p.chunks + p.devices + s * quads
             field_ref[to : to + quads, :] = fields[first : first + quads]
+    fill_slots(p, me_ref, recv_ref, place_ref)
     for copy in copies:
         copy.wait()
 
@@ -383,86 +446,52 @@
     ] + [pltpu.SMEM((8, p.padded), jnp.int32)] * 16 + [pltpu.VMEM((p.cols * LANES, LANES), jnp.float32) for _ in range(2 * BATCH)]
 
 
-def slots_kernel(plan, me_ref, recv_ref, out_ref):
-    p = plan
-    table_at, scal_at = me_ref[0], me_ref[1]
-    half_x = p.nx // 2
-    width = LG * half_x
-    codes = recv_ref[pl.ds(scal_at * 8 + 7, p.table, stride=8 * p.scal), :].astype(jnp.bfloat16)
-    step = 2 * LANES
-    for h in range(2):
-        x = iota((1, width), 1) % half_x + h * half_x
-        inside = (iota((1, width), 1) // half_x) * BX + x % BX + GROUP * (table_at % 2)
-        move = (iota((LANES, width), 0) == inside).astype(jnp.float32).astype(jnp.bfloat16)
-        moved = jnp.dot(codes, move, preferred_element_type=jnp.float32)
-        t = x // BX
-        moved = jnp.where(iota((p.table, width), 0) == t, moved, 0.0)
-        code = jnp.sum(moved, axis=0, keepdims=True).astype(jnp.int32)
-        shard, slot = code // p.code, code % p.code
-        t = t - h * (p.table // 2)
-        near = (shard // 2) * LANES + (shard % 2) * GROUP + t * p.near + slot
-        quad = shard // 4
-        far = (p.table // 2 + quad // 2) * LANES + (quad % 2) * GROUP
-        far = far + t * p.quad + (shard % 4) * p.far + slot - p.near
-        chosen = jnp.where(slot < p.near, near, far)
-        rows = iota((step, width), 0)
-
-        def fill(i, carry):
-            start = pl.multiple_of(i * step, step)
-            hit = rows == chosen - start
-            out_ref[h, pl.ds(start, step), :] = jnp.where(hit, 1.0, 0.0).astype(jnp.bfloat16)
-            return carry
-
-        lax.fori_loop(0, out_ref.shape[1] // step, fill, 0)
-
-
 def filter_kernel(plan, recv_ref, place_ref, op_ref, filtered_ref, gradient_ref, *left_refs):
     p = plan
-    lane = iota((1, LANES), 1)
-    low = lane < GROUP
-    quad_of = (lane // p.far) % 4
-
-    def halves(first, second, rows, col):
-        turned = [pltpu.roll(tile, GROUP, 1) for tile in (first, second)]
-        left_refs[0][rows, col : col + LANES] = jnp.where(low, first, turned[1])
-        left_refs[1][rows, col : col + LANES] = jnp.where(low, turned[0], second)
-
-    for o in range(0, p.table, 2):
-        for sc in range(p.scal):
+    quad_of = (iota((1, LANES), 1) // p.far) % 4
+
+    def put(tiles, first_row, col):
+        for left_ref, tile in zip(left_refs, swap_four(tiles), strict=True):
+            left_ref[first_row : first_row + tile.shape[0], col : col + LANES] = tile
+
+    for sc in range(p.scal):
+        for o in range(0, p.table, 4):
+            starts = [((o + i) * p.scal + sc) * p.rows for i in range(4)]
+            tiles = [recv_ref[start : start + p.scalars, :] for start in starts]
+            put(tiles, sc * p.scalars, o // 4 * LANES)
+        for quad in range(0, p.table // 4, 4):
             tiles = []
-            for i in range(2):
-                start = ((o + i) * p.scal + sc) * p.rows
-                tiles.append(recv_ref[start : start + p.scalars, :])
-            halves(*tiles, slice(sc * p.scalars, (sc + 1) * p.scalars), o // 2 * LANES)
-    for quad in range(0, p.table // 4, 2):
-        for sc in range(p.scal):
-            for b in range(4):
-                parts = []
-                for n in range(2):
+            for n in range(4):
+                starts = [((quad + n) * 4 + i) * p.scal + sc for i in range(4)]
+                starts = [start * p.rows + p.scalars for start in starts]
+                tile = []
+                for b in range(4):
                     part = jnp.zeros((p.few, LANES), jnp.float32)
                     for i in range(4):
-                        start = (((quad + n) * 4 + i) * p.scal + sc) * p.rows + p.scalars
-                        turned = recv_ref[start : start + p.few, :]
+                        turned = recv_ref[starts[i] : starts[i] + p.few, :]
                         turned = pltpu.roll(turned, ((i - b) * p.far) % LANES, 1)
                         part = jnp.where(quad_of == i, turned, part)
-                    parts.append(part)
-                row = sc * p.scalars + b * p.few
-                halves(*parts, slice(row, row + p.few), (p.table + quad) // 2 * LANES)
+                    tile.append(part)
+                tiles.append(jnp.concatenate(tile, axis=0))
+            put(tiles, sc * p.scalars, (p.table // 4 + quad // 4) * LANES)
     sides = []
-    for h in range(2):
+    for h in range(4):
         left = jnp.concatenate(pieces_of(left_refs[h][...], 3), axis=0)
         values = jnp.dot(left, place_ref[h], preferred_element_type=jnp.float32)
         sides.append(
             values[0:SCAL_ALL] + values[SCAL_ALL : 2 * SCAL_ALL] + values[2 * SCAL_ALL :]
         )
-    half_x = p.nx // 2
-    lines = jnp.concatenate(
-        [
-            jnp.concatenate([side[:, r * half_x : (r + 1) * half_x] for side in sides], axis=1)
+    part_x = p.nx // 4
+    if part_x == 32:
+        lines = []
+        for first in range(0, LG * part_x, LANES):
+            lines.extend(swap_four([side[:, first : first + LANES] for side in sides]))
+    else:
+        lines = [
+            jnp.concatenate([side[:, r * part_x : (r + 1) * part_x] for side in sides], axis=1)
             for r in range(LG)
-        ],
-        axis=0,
-    )
+        ]
+    lines = jnp.concatenate(lines, axis=0)
     both = jnp.dot(
         lines, op_ref[...], precision=lax.Precision.HIGHEST, preferred_element_type=jnp.float32
     )
@@ -504,65 +533,61 @@
     row_count = p.cells // LANES
     owners = owner_shard.reshape(row_count, LANES)
     bins = local_bin.reshape(row_count, LANES)
-    requests = call(
+    bin_count, depth = flamelet_table.shape
+    table = flamelet_table.reshape(bin_count // 8, 8, p.cols, LANES).transpose(0, 2, 1, 3)
+    table = table.reshape(bin_count * p.cols, LANES)
+    requests, early = call(
         request_kernel,
         p,
-        jax.ShapeDtypeStruct((p.devices, 8, LANES), f32),
-        [HBM] * 3,
+        (
+            jax.ShapeDtypeStruct((p.devices, 8, LANES), f32),
+            jax.ShapeDtypeStruct((bin_count * p.cols * 11 // 32, LANES), f32),
+        ),
+        [HBM] * 4,
         [
             pltpu.VMEM((8, p.cells), f32),
             pltpu.VMEM(cell_coords.shape, f32),
             pltpu.VMEM(owners.shape, i32),
             pltpu.VMEM(bins.shape, i32),
-            pltpu.SemaphoreType.DMA((3,)),
+            pltpu.SemaphoreType.DMA((4,)),
         ],
-        60,
+        32,
         1 << 20,
         "requests",
-    )(cell_coords, owners, bins)
+    )(*[pltpu.with_memory_space_constraint(a, pltpu.HBM) for a in (cell_coords, owners, bins, table)])
+    me = jnp.stack([lax.axis_index("table"), lax.axis_index("scal")]).astype(i32)
+    me, requests = lax.optimization_barrier((me, requests))
     received = exchange(requests).reshape(p.devices * 8, LANES)
-
-    bin_count, depth = flamelet_table.shape
-    table = flamelet_table.reshape(bin_count // 8, 8, p.cols, LANES).transpose(0, 2, 1, 3)
-    table = table.reshape(bin_count * p.cols, LANES)
-    early = table[: bin_count * p.cols * 11 // 32]
-    replies = call(
+    replies, place = call(
         lookup_kernel,
         p,
-        jax.ShapeDtypeStruct((p.devices * p.rows, LANES), f32),
-        [VMEM, VMEM, HBM],
+        (
+            jax.ShapeDtypeStruct((p.devices * p.rows, LANES), f32),
+            jax.ShapeDtypeStruct((4, p.table * 5 * LANES // 16, LG * p.nx // 4), jnp.bfloat16),
+        ),
+        [SMEM, VMEM, VMEM, HBM],
         lookup_scratch(p, table.shape),
-        50,
+        30,
         1 << 24,
         "lookup",
-    )(received, early, table)
+    )(me, received, early, pltpu.with_memory_space_constraint(table, pltpu.HBM))
     answers = exchange(replies.reshape(p.devices, 1, p.rows * LANES))
     answers = answers.reshape(p.devices * p.rows, LANES)
 
-    me = jnp.stack([lax.axis_index("table"), lax.axis_index("scal")]).astype(i32)
-    place = call(
-        slots_kernel,
-        p,
-        jax.ShapeDtypeStruct((2, p.table * 5 * LANES // 8, LG * p.nx // 2), jnp.bfloat16),
-        [SMEM, VMEM],
-        [],
-        8 + p.nx * p.table // 128,
-        1 << 24,
-        "slots",
-    )(me, received)
     filter_op = filter_table(p.nx).T
     both_op = np.concatenate([filter_op, filter_op @ derivative_table(p.nx).T], axis=1)
+    both_op = jnp.asarray(both_op.astype(np.float32))
     out = jax.ShapeDtypeStruct((p.nx // LANES * SCAL_ALL * LG, LANES), f32)
     outs = call(
         filter_kernel,
         p,
         (out, out),
         [VMEM] * 3,
-        [pltpu.VMEM((SCAL_ALL, p.table * 5 * LANES // 8), f32)] * 2,
+        [pltpu.VMEM((SCAL_ALL, p.table * 5 * LANES // 16), f32)] * 4,
         8 + p.nx * p.table // 64,
         1 << 24,
         "filter",
-    )(answers, place, jnp.asarray(both_op.astype(np.float32)))
+    )(answers, place, both_op)
     outs = [out.reshape(p.nx // LANES, SCAL_ALL, LG, LANES).transpose(1, 2, 0, 3) for out in outs]
     return tuple(out.reshape(SCAL_ALL, LG, p.nx) for out in outs)
 

time: 44.2 us -> 42.6 us (0.964)
  blocking collectives: 0 us -> 29.2 us
  waiting for transfers between devices: 16.6 us -> 0 us
  starting transfers between devices: 10 us -> 0 us
  local copies, waits for them, and re-layouts: 2.1 us -> 0.01 us
  Pallas kernels: 14.2 us -> 12.4 us
    all_to_all x0 -> x2, blocking collectives: none -> 29.2 us  [exchange(): return lax.all_to_all(array, AXES, split_axis=0, concat_axis=0, tiled=True)]
    all_to_all x2 -> x0, waiting for transfers between devices: 16.6 us -> none  [exchange(): return lax.all_to_all(array, AXES, split_axis=0, concat_axis=0, tiled=True)]
    all_to_all x2 -> x0, starting transfers between devices: 10 us -> none  [exchange(): return lax.all_to_all(array, AXES, split_axis=0, concat_axis=0, tiled=True)]
    slice x1 -> x0, local copies, waits for them, and re-layouts: 2.09 us -> none  [on_device(): early = table[:bin_count * p.cols * 11 // 32]]
    pallas_call x3 -> x2, Pallas kernels: 12.5 us -> 10.6 us  [the longest x1 8.73 us: on_device(): call(lookup_kernel, p, (jax.ShapeDtypeStruct((p.devices * p.rows, LANES),...]
  transfers between devices with their start and end apart: 2 -> 0, of which waited for: 2 -> 0; matrix products, arithmetic and copies ran while one was open for 5% -> 0% of each run, Pallas kernels for 3% -> 0%
where the time goes in v6:
time: 42.6 us; the launch traced here: 42.3 us
  blocking collectives  29.2 us (69%)
  Pallas kernels  12.4 us (29%)
  between operations  0.65 us (2%)
    all_to_all x2, blocking collectives, exchange(): return lax.all_to_all(array, AXES, split_axis=0, concat_axis=0, tiled=True)  29.2 us
    pallas_call x1, Pallas kernels, on_device(): call(lookup_kernel, p, (jax.ShapeDtypeStruct((p.devices * p.rows, LANES),...  8.73 us
    pallas_call x1, Pallas kernels, on_device(): call(request_kernel, p, (jax.ShapeDtypeStruct((p.devices, 8, LANES), f32)...  1.9 us
    pallas_call x1, Pallas kernels, on_device(): call(filter_kernel, p, (out, out), [VMEM] * 3, [pltpu.VMEM((SCAL_ALL, p.t...  1.8 us

profile of v6, /device:TPU:0, one launch (start us, length us, event | category | flops | bytes accessed | tf_op | source)
XLA Modules:
  0.0 42.3 jit_solution(4950906703635228314)
XLA Ops:
  0.6 0.1 pad_add_fusion.me_ref
  0.7 1.9 %requests.1 = (f32[32,8,128]{2,1,0:T(8,128)S(1)}, f32[5632,128]{1,0:T(8,128)S(1)}) custom-call(f32[4,1024]{1,0:T(4,128)} %coords_in.1, s32[8,128]{1,0:T(8,128)} %bitcast.19, s32[8,128]{1,0:T(8,128)} %bitcast.20, f32[16384,128]{1,0:T(8,128)} %bitcast.17), custom_call_target="tpu_custom_call" | custom-call | flops 1048576 | bytes 4096 | tf_op jit(solution)/shard_map/requests/pallas_call | solution.py:539
  2.6 15.7 %all_to_all.10 = f32[32,8,128]{2,1,0:T(8,128)S(1)} all-to-all(f32[32,8,128]{2,1,0:T(8,128)S(1)} %get-tuple-element.12), channel_id=1, replica_groups=mesh['table'=16,'scal'=2] {'table','scal'}, dimensions={0} | all-to-all | bytes 262144 | tf_op jit(solution)/shard_map/all_to_all | solution.py:527
  18.3 0.0 copy-start
  18.3 8.7 %lookup.1 = (f32[640,128]{1,0:T(8,128)S(1)}, bf16[4,640,256]{2,1,0:T(8,128)(2,1)S(1)}) custom-call(s32[2]{0:T(128)S(1)} %pad_add_fusion.me_ref, f32[256,128]{1,0:T(8,128)S(1)} %bitcast.15, f32[5632,128]{1,0:T(8,128)S(1)} %get-tuple-element.13.early_ref, f32[16384,128]{1,0:T(8,128)} %bitcast.18), custom_call_target="tpu_custom_call" | custom-call | flops 16777216 | bytes 65536 | tf_op jit(solution)/shard_map/lookup/pallas_call | solution.py:561
  27.1 13.4 %all_to_all.11 = f32[32,1,2560]{2,1,0:T(1,128)S(1)} all-to-all(f32[32,1,2560]{2,1,0:T(1,128)S(1)} %bitcast.16), channel_id=1, replica_groups=mesh['table'=16,'scal'=2] {'table','scal'}, dimensions={0} | all-to-all | bytes 655360 | tf_op jit(solution)/shard_map/all_to_all | solution.py:527
  40.5 0.0 copy-done
  40.5 1.8 %filter.1 = (f32[256,128]{1,0:T(8,128)}, f32[256,128]{1,0:T(8,128)}) custom-call(f32[640,128]{1,0:T(8,128)S(1)} %bitcast.14, bf16[4,640,256]{2,1,0:T(8,128)(2,1)S(1)} %get-tuple-element.15.place_ref, f32[128,256]{1,0:T(8,128)S(1)} %copy-done), custom_call_target="tpu_custom_call" | custom-call | flops 16777216 | bytes 65536 | tf_op jit(solution)/shard_map/filter/pallas_call | solution.py:581
Async XLA Ops:
  18.3 22.2 %copy-start = (f32[128,256]{1,0:T(8,128)S(1)}, f32[128,256]{1,0:T(8,128)}, u32[]{:S(2)}) copy-start(f32[128,256]{1,0:T(8,128)} %constant.10.clone.op_ref) | copy-start | bytes 393220

commit v7 on v6

--- a/solution.py
+++ b/solution.py
@@ -247,9 +247,9 @@
     return x
 
 
-def fill_slots(plan, me_ref, recv_ref, out_ref):
+def fill_slots(plan, recv_ref, out_ref):
     p = plan
-    table_at, scal_at = me_ref[0], me_ref[1]
+    table_at, scal_at = lax.axis_index("table"), lax.axis_index("scal")
     part_x = p.nx // 4
     width = LG * part_x
     codes = recv_ref[pl.ds(scal_at * 8 + 7, p.table, stride=8 * p.scal), :].astype(jnp.bfloat16)
@@ -292,7 +292,6 @@
 
 def lookup_kernel(
     plan,
-    me_ref,
     recv_ref,
     early_ref,
     table_in,
@@ -357,7 +356,7 @@
             first = 4 * p.devices + s * p.table + f * quads
             to = f * p.chunks + p.devices + s * quads
             field_ref[to : to + quads, :] = fields[first : first + quads]
-    fill_slots(p, me_ref, recv_ref, place_ref)
+    fill_slots(p, recv_ref, place_ref)
     for copy in copies:
         copy.wait()
 
@@ -492,8 +491,11 @@
             for r in range(LG)
         ]
     lines = jnp.concatenate(lines, axis=0)
+    lines, op = pieces_of(lines, 2), pieces_of(op_ref[...], 2)
     both = jnp.dot(
-        lines, op_ref[...], precision=lax.Precision.HIGHEST, preferred_element_type=jnp.float32
+        jnp.concatenate([lines[0], lines[0], lines[1]], axis=1),
+        jnp.concatenate([op[0], op[1], op[0]], axis=0),
+        preferred_element_type=jnp.float32,
     )
     for r in range(LG):
         rows = slice(r * SCAL_ALL, (r + 1) * SCAL_ALL)
@@ -555,8 +557,6 @@
         1 << 20,
         "requests",
     )(*[pltpu.with_memory_space_constraint(a, pltpu.HBM) for a in (cell_coords, owners, bins, table)])
-    me = jnp.stack([lax.axis_index("table"), lax.axis_index("scal")]).astype(i32)
-    me, requests = lax.optimization_barrier((me, requests))
     received = exchange(requests).reshape(p.devices * 8, LANES)
     replies, place = call(
         lookup_kernel,
@@ -565,12 +565,12 @@
             jax.ShapeDtypeStruct((p.devices * p.rows, LANES), f32),
             jax.ShapeDtypeStruct((4, p.table * 5 * LANES // 16, LG * p.nx // 4), jnp.bfloat16),
         ),
-        [SMEM, VMEM, VMEM, HBM],
+        [VMEM, VMEM, HBM],
         lookup_scratch(p, table.shape),
         30,
         1 << 24,
         "lookup",
-    )(me, received, early, pltpu.with_memory_space_constraint(table, pltpu.HBM))
+    )(received, early, pltpu.with_memory_space_constraint(table, pltpu.HBM))
     answers = exchange(replies.reshape(p.devices, 1, p.rows * LANES))
     answers = answers.reshape(p.devices * p.rows, LANES)
 

time: 42.6 us -> 41.8 us (0.981)
  Pallas kernels: 12.4 us -> 11.8 us
    pallas_call x1, Pallas kernels: 8.73 us -> 8.22 us  [on_device(): call(lookup_kernel, p, (jax.ShapeDtypeStruct((p.devices * p.rows, LANES),...]
where the time goes in v7:
time: 41.8 us; the launch traced here: 41.6 us
  blocking collectives  29.2 us (70%)
  Pallas kernels  11.8 us (28%)
  between operations  0.65 us (2%)
    all_to_all x2, blocking collectives, exchange(): return lax.all_to_all(array, AXES, split_axis=0, concat_axis=0, tiled=True)  29.2 us
    pallas_call x1, Pallas kernels, on_device(): call(lookup_kernel, p, (jax.ShapeDtypeStruct((p.devices * p.rows, LANES),...  8.22 us
    pallas_call x1, Pallas kernels, on_device(): call(request_kernel, p, (jax.ShapeDtypeStruct((p.devices, 8, LANES), f32)...  1.9 us
    pallas_call x1, Pallas kernels, on_device(): call(filter_kernel, p, (out, out), [VMEM] * 3, [pltpu.VMEM((SCAL_ALL, p.t...  1.68 us

profile of v7, /device:TPU:0, one launch (start us, length us, event | category | flops | bytes accessed | tf_op | source)
XLA Modules:
  0.0 41.6 jit_solution(14648337987639830834)
XLA Ops:
  0.6 1.9 %requests.1 = (f32[32,8,128]{2,1,0:T(8,128)S(1)}, f32[5632,128]{1,0:T(8,128)S(1)}) custom-call(f32[4,1024]{1,0:T(4,128)} %coords_in.1, s32[8,128]{1,0:T(8,128)} %bitcast.17, s32[8,128]{1,0:T(8,128)} %bitcast.18, f32[16384,128]{1,0:T(8,128)} %bitcast.15), custom_call_target="tpu_custom_call" | custom-call | flops 1048576 | bytes 4096 | tf_op jit(solution)/shard_map/requests/pallas_call | solution.py:541
  2.5 15.7 %all_to_all.10 = f32[32,8,128]{2,1,0:T(8,128)S(1)} all-to-all(f32[32,8,128]{2,1,0:T(8,128)S(1)} %get-tuple-element.8), channel_id=1, replica_groups=mesh['table'=16,'scal'=2] {'table','scal'}, dimensions={0} | all-to-all | bytes 262144 | tf_op jit(solution)/shard_map/all_to_all | solution.py:529
  18.3 0.0 copy-start
  18.3 8.2 %lookup.1 = (f32[640,128]{1,0:T(8,128)S(1)}, bf16[4,640,256]{2,1,0:T(8,128)(2,1)S(1)}) custom-call(f32[256,128]{1,0:T(8,128)S(1)} %bitcast.13, f32[5632,128]{1,0:T(8,128)S(1)} %get-tuple-element.9.early_ref, f32[16384,128]{1,0:T(8,128)} %bitcast.16), custom_call_target="tpu_custom_call" | custom-call | flops 16777216 | bytes 65536 | tf_op jit(solution)/shard_map/lookup/pallas_call | solution.py:561
  26.5 13.4 %all_to_all.11 = f32[32,1,2560]{2,1,0:T(1,128)S(1)} all-to-all(f32[32,1,2560]{2,1,0:T(1,128)S(1)} %bitcast.14), channel_id=1, replica_groups=mesh['table'=16,'scal'=2] {'table','scal'}, dimensions={0} | all-to-all | bytes 655360 | tf_op jit(solution)/shard_map/all_to_all | solution.py:529
  39.9 0.0 copy-done
  39.9 1.7 %filter.1 = (f32[256,128]{1,0:T(8,128)}, f32[256,128]{1,0:T(8,128)}) custom-call(f32[640,128]{1,0:T(8,128)S(1)} %bitcast.12, bf16[4,640,256]{2,1,0:T(8,128)(2,1)S(1)} %get-tuple-element.11.place_ref, f32[128,256]{1,0:T(8,128)S(1)} %copy-done), custom_call_target="tpu_custom_call" | custom-call | flops 16777216 | bytes 65536 | tf_op jit(solution)/shard_map/filter/pallas_call | solution.py:581
Async XLA Ops:
  18.3 21.7 %copy-start = (f32[128,256]{1,0:T(8,128)S(1)}, f32[128,256]{1,0:T(8,128)}, u32[]{:S(2)}) copy-start(f32[128,256]{1,0:T(8,128)} %constant.2.clone.op_ref) | copy-start | bytes 393220

commit v8 on v7

--- a/solution.py
+++ b/solution.py
@@ -362,14 +362,15 @@
 
     def fetch(store, chunk, part):
         step = LANES // p.cols
-        for slot in range(part * step, (part + 1) * step):
-            address = idx_refs[slot // 8][slot % 8, chunk]
-            if p.cols == 1:
-                store[slot : slot + 1, :] = table_ref[pl.ds(address, 1), :]
-            else:
-                store[slot * p.cols : (slot + 1) * p.cols, :] = table_ref[
-                    pl.ds(address, p.cols, stride=8), :
-                ]
+        for slot in range(part * step, (part + 1) * step, 2):
+            rows = []
+            for i in (slot, slot + 1):
+                address = idx_refs[i // 8][i % 8, chunk]
+                if p.cols == 1:
+                    rows.append(table_ref[pl.ds(address, 1), :])
+                else:
+                    rows.append(table_ref[pl.ds(address, p.cols, stride=8), :])
+            store[slot * p.cols : (slot + 2) * p.cols, :] = jnp.concatenate(rows, axis=0)
 
     def reduce(store, chunk, ahead=None):
         weights = spline_rows([field_ref[pl.ds(f * p.chunks + chunk, 1), :] for f in range(4)])

time: 41.8 us -> 41.3 us (0.988)
  Pallas kernels: 11.8 us -> 11.2 us
    pallas_call x1, Pallas kernels: 8.22 us -> 7.66 us  [on_device(): call(lookup_kernel, p, (jax.ShapeDtypeStruct((p.devices * p.rows, LANES),...]
where the time goes in v8:
time: 41.3 us; the launch traced here: 41 us
  blocking collectives  29.2 us (71%)
  Pallas kernels  11.2 us (27%)
  between operations  0.65 us (2%)
    all_to_all x2, blocking collectives, exchange(): return lax.all_to_all(array, AXES, split_axis=0, concat_axis=0, tiled=True)  29.2 us
    pallas_call x1, Pallas kernels, on_device(): call(lookup_kernel, p, (jax.ShapeDtypeStruct((p.devices * p.rows, LANES),...  7.66 us
    pallas_call x1, Pallas kernels, on_device(): call(request_kernel, p, (jax.ShapeDtypeStruct((p.devices, 8, LANES), f32)...  1.9 us
    pallas_call x1, Pallas kernels, on_device(): call(filter_kernel, p, (out, out), [VMEM] * 3, [pltpu.VMEM((SCAL_ALL, p.t...  1.68 us

profile of v8, /device:TPU:0, one launch (start us, length us, event | category | flops | bytes accessed | tf_op | source)
XLA Modules:
  0.0 41.0 jit_solution(4591794965887231415)
XLA Ops:
  0.6 1.9 %requests.1 = (f32[32,8,128]{2,1,0:T(8,128)S(1)}, f32[5632,128]{1,0:T(8,128)S(1)}) custom-call(f32[4,1024]{1,0:T(4,128)} %coords_in.1, s32[8,128]{1,0:T(8,128)} %bitcast.17, s32[8,128]{1,0:T(8,128)} %bitcast.18, f32[16384,128]{1,0:T(8,128)} %bitcast.15), custom_call_target="tpu_custom_call" | custom-call | flops 1048576 | bytes 4096 | tf_op jit(solution)/shard_map/requests/pallas_call | solution.py:542
  2.5 15.7 %all_to_all.10 = f32[32,8,128]{2,1,0:T(8,128)S(1)} all-to-all(f32[32,8,128]{2,1,0:T(8,128)S(1)} %get-tuple-element.8), channel_id=1, replica_groups=mesh['table'=16,'scal'=2] {'table','scal'}, dimensions={0} | all-to-all | bytes 262144 | tf_op jit(solution)/shard_map/all_to_all | solution.py:530
  18.3 0.0 copy-start
  18.3 7.7 %lookup.1 = (f32[640,128]{1,0:T(8,128)S(1)}, bf16[4,640,256]{2,1,0:T(8,128)(2,1)S(1)}) custom-call(f32[256,128]{1,0:T(8,128)S(1)} %bitcast.13, f32[5632,128]{1,0:T(8,128)S(1)} %get-tuple-element.9.early_ref, f32[16384,128]{1,0:T(8,128)} %bitcast.16), custom_call_target="tpu_custom_call" | custom-call | flops 16777216 | bytes 65536 | tf_op jit(solution)/shard_map/lookup/pallas_call | solution.py:562
  25.9 13.4 %all_to_all.11 = f32[32,1,2560]{2,1,0:T(1,128)S(1)} all-to-all(f32[32,1,2560]{2,1,0:T(1,128)S(1)} %bitcast.14), channel_id=1, replica_groups=mesh['table'=16,'scal'=2] {'table','scal'}, dimensions={0} | all-to-all | bytes 655360 | tf_op jit(solution)/shard_map/all_to_all | solution.py:530
  39.4 0.0 copy-done
  39.4 1.7 %filter.1 = (f32[256,128]{1,0:T(8,128)}, f32[256,128]{1,0:T(8,128)}) custom-call(f32[640,128]{1,0:T(8,128)S(1)} %bitcast.12, bf16[4,640,256]{2,1,0:T(8,128)(2,1)S(1)} %get-tuple-element.11.place_ref, f32[128,256]{1,0:T(8,128)S(1)} %copy-done), custom_call_target="tpu_custom_call" | custom-call | flops 16777216 | bytes 65536 | tf_op jit(solution)/shard_map/filter/pallas_call | solution.py:582
Async XLA Ops:
  18.3 21.1 %copy-start = (f32[128,256]{1,0:T(8,128)S(1)}, f32[128,256]{1,0:T(8,128)}, u32[]{:S(2)}) copy-start(f32[128,256]{1,0:T(8,128)} %constant.2.clone.op_ref) | copy-start | bytes 393220

commit v9 on v8

--- a/solution.py
+++ b/solution.py
@@ -16,6 +16,7 @@
 LANES = 128
 AXES = ("table", "scal")
 BATCH = 4
+SENT = 7
 
 strength = 0.499
 
@@ -199,17 +200,20 @@
     placed = placed[0:total] + placed[total : 2 * total] + placed[2 * total :]
     sub = iota((8, LANES), 0)
     block = iota((8, LANES), 1) // 32
+    upper = iota((1, LANES), 1) >= GROUP
     for o in range(p.table):
         near_part = placed[o * 8 : (o + 1) * 8, :LANES]
         far_part = placed[o * 8 : (o + 1) * 8, LANES:]
         far_coords = jnp.sum(jnp.where(sub == block, far_part, 0.0), axis=0, keepdims=True)
+        code = codes[o // 2] if o % 2 else pltpu.roll(codes[o // 2], GROUP, 1)
         message = jnp.where(
             sub < 5,
             near_part,
-            jnp.where(sub == 5, far_coords, jnp.where(sub == 6, far_part[4:5], codes[o // 2])),
+            jnp.where(sub == 5, far_coords, jnp.where(upper, code, far_part[4:5])),
         )
         for sc in range(p.scal):
-            out_ref[o * p.scal + sc] = message
+            start = (o * p.scal + sc) * SENT
+            out_ref[start : start + SENT, :] = message[:SENT]
     early.wait()
 
 
@@ -249,14 +253,18 @@
 
 def fill_slots(plan, recv_ref, out_ref):
     p = plan
-    table_at, scal_at = lax.axis_index("table"), lax.axis_index("scal")
+    scal_at = lax.axis_index("scal")
     part_x = p.nx // 4
     width = LG * part_x
-    codes = recv_ref[pl.ds(scal_at * 8 + 7, p.table, stride=8 * p.scal), :].astype(jnp.bfloat16)
+    codes = jnp.zeros((p.table, LANES), jnp.float32)
+    for s in range(p.scal):
+        rows = recv_ref[pl.ds(s * SENT + 6, p.table, stride=SENT * p.scal), :]
+        codes = jnp.where(scal_at == s, rows, codes)
+    codes = codes.astype(jnp.bfloat16)
     step = LANES
     for h in range(4):
         x = iota((1, width), 1) % part_x + h * part_x
-        inside = (iota((1, width), 1) // part_x) * BX + x % BX + GROUP * (table_at % 2)
+        inside = (iota((1, width), 1) // part_x) * BX + x % BX + GROUP
         move = (iota((LANES, width), 0) == inside).astype(jnp.float32).astype(jnp.bfloat16)
         moved = jnp.dot(codes, move, preferred_element_type=jnp.float32)
         t = x // BX
@@ -308,7 +316,7 @@
     idx_refs, stores = rest[:16], rest[16:]
     quads = p.table // 4
     early = early_ref.shape[0]
-    late = table_ref.shape[0] - early
+    late = table_in.shape[0] - early
     loads = [
         pltpu.make_async_copy(
             table_in.at[pl.ds(early, late // 2)], table_ref.at[pl.ds(early, late // 2)], sem.at[1]
@@ -323,7 +331,7 @@
     loads[0].start()
 
     def received(r):
-        rows = [recv_ref[pl.ds(s * 8 + r, p.table, stride=8 * p.scal), :] for s in range(p.scal)]
+        rows = [recv_ref[pl.ds(s * SENT + r, p.table, stride=SENT * p.scal), :] for s in range(p.scal)]
         return jnp.concatenate(rows, axis=0)
 
     addresses = jnp.concatenate([received(4), received(6)], axis=0)
@@ -438,7 +446,7 @@
 def lookup_scratch(plan, table_shape):
     p = plan
     return [
-        pltpu.VMEM(table_shape, jnp.float32),
+        pltpu.VMEM((table_shape[0] + 8 * p.cols, LANES), jnp.float32),
         pltpu.VMEM((LANES, p.padded), jnp.int32),
         pltpu.VMEM((4 * p.chunks, LANES), jnp.float32),
         pltpu.VMEM((p.chunks * p.scalars, LANES), jnp.float32),
@@ -543,7 +551,7 @@
         request_kernel,
         p,
         (
-            jax.ShapeDtypeStruct((p.devices, 8, LANES), f32),
+            jax.ShapeDtypeStruct((p.devices * SENT, LANES), f32),
             jax.ShapeDtypeStruct((bin_count * p.cols * 11 // 32, LANES), f32),
         ),
         [HBM] * 4,
@@ -558,7 +566,8 @@
         1 << 20,
         "requests",
     )(*[pltpu.with_memory_space_constraint(a, pltpu.HBM) for a in (cell_coords, owners, bins, table)])
-    received = exchange(requests).reshape(p.devices * 8, LANES)
+    received = exchange(requests.reshape(p.devices, 1, SENT * LANES))
+    received = received.reshape(p.devices * SENT, LANES)
     replies, place = call(
         lookup_kernel,
         p,

time: 41.3 us -> 41 us (level)
  no operation moved by 1% of the time
where the time goes in v9:
time: 41 us; the launch traced here: 40.8 us
  blocking collectives  28.9 us (70%)
  Pallas kernels  11.2 us (27%)
  between operations  0.65 us (2%)
    all_to_all x2, blocking collectives, exchange(): return lax.all_to_all(array, AXES, split_axis=0, concat_axis=0, tiled=True)  28.9 us
    pallas_call x1, Pallas kernels, on_device(): call(lookup_kernel, p, (jax.ShapeDtypeStruct((p.devices * p.rows, LANES),...  7.65 us
    pallas_call x1, Pallas kernels, on_device(): call(request_kernel, p, (jax.ShapeDtypeStruct((p.devices * SENT, LANES),...  1.9 us
    pallas_call x1, Pallas kernels, on_device(): call(filter_kernel, p, (out, out), [VMEM] * 3, [pltpu.VMEM((SCAL_ALL, p.t...  1.68 us

profile of v9, /device:TPU:0, one launch (start us, length us, event | category | flops | bytes accessed | tf_op | source)
XLA Modules:
  0.0 40.8 jit_solution(7567321462992800271)
XLA Ops:
  0.6 1.9 %requests.1 = (f32[224,128]{1,0:T(8,128)S(1)}, f32[5632,128]{1,0:T(8,128)S(1)}) custom-call(f32[4,1024]{1,0:T(4,128)} %coords_in.1, s32[8,128]{1,0:T(8,128)} %bitcast.19, s32[8,128]{1,0:T(8,128)} %bitcast.20, f32[16384,128]{1,0:T(8,128)} %bitcast.17), custom_call_target="tpu_custom_call" | custom-call | flops 1048576 | bytes 4096 | tf_op jit(solution)/shard_map/requests/pallas_call | solution.py:550
  2.5 15.5 %all_to_all.10 = f32[32,1,896]{2,1,0:T(1,128)S(1)} all-to-all(f32[32,1,896]{2,1,0:T(1,128)S(1)} %bitcast.16), channel_id=1, replica_groups=mesh['table'=16,'scal'=2] {'table','scal'}, dimensions={0} | all-to-all | bytes 229376 | tf_op jit(solution)/shard_map/all_to_all | solution.py:538
  18.0 0.0 copy-start
  18.0 7.6 %lookup.1 = (f32[640,128]{1,0:T(8,128)S(1)}, bf16[4,640,256]{2,1,0:T(8,128)(2,1)S(1)}) custom-call(f32[224,128]{1,0:T(8,128)S(1)} %bitcast.14, f32[5632,128]{1,0:T(8,128)S(1)} %get-tuple-element.9.early_ref, f32[16384,128]{1,0:T(8,128)} %bitcast.18), custom_call_target="tpu_custom_call" | custom-call | flops 16777216 | bytes 65536 | tf_op jit(solution)/shard_map/lookup/pallas_call | solution.py:571
  25.7 13.4 %all_to_all.11 = f32[32,1,2560]{2,1,0:T(1,128)S(1)} all-to-all(f32[32,1,2560]{2,1,0:T(1,128)S(1)} %bitcast.15), channel_id=1, replica_groups=mesh['table'=16,'scal'=2] {'table','scal'}, dimensions={0} | all-to-all | bytes 655360 | tf_op jit(solution)/shard_map/all_to_all | solution.py:538
  39.1 0.0 copy-done
  39.1 1.7 %filter.1 = (f32[256,128]{1,0:T(8,128)}, f32[256,128]{1,0:T(8,128)}) custom-call(f32[640,128]{1,0:T(8,128)S(1)} %bitcast.13, bf16[4,640,256]{2,1,0:T(8,128)(2,1)S(1)} %get-tuple-element.11.place_ref, f32[128,256]{1,0:T(8,128)S(1)} %copy-done), custom_call_target="tpu_custom_call" | custom-call | flops 16777216 | bytes 65536 | tf_op jit(solution)/shard_map/filter/pallas_call | solution.py:591
Async XLA Ops:
  18.0 21.1 %copy-start = (f32[128,256]{1,0:T(8,128)S(1)}, f32[128,256]{1,0:T(8,128)}, u32[]{:S(2)}) copy-start(f32[128,256]{1,0:T(8,128)} %constant.2.clone.op_ref) | copy-start | bytes 393220

commit v10 on v9

--- a/solution.py
+++ b/solution.py
@@ -212,7 +212,7 @@
             jnp.where(sub == 5, far_coords, jnp.where(upper, code, far_part[4:5])),
         )
         for sc in range(p.scal):
-            start = (o * p.scal + sc) * SENT
+            start = (sc * p.table + o) * SENT
             out_ref[start : start + SENT, :] = message[:SENT]
     early.wait()
 
@@ -258,7 +258,7 @@
     width = LG * part_x
     codes = jnp.zeros((p.table, LANES), jnp.float32)
     for s in range(p.scal):
-        rows = recv_ref[pl.ds(s * SENT + 6, p.table, stride=SENT * p.scal), :]
+        rows = recv_ref[pl.ds(s * p.table * SENT + 6, p.table, stride=SENT), :]
         codes = jnp.where(scal_at == s, rows, codes)
     codes = codes.astype(jnp.bfloat16)
     step = LANES
@@ -331,7 +331,7 @@
     loads[0].start()
 
     def received(r):
-        rows = [recv_ref[pl.ds(s * SENT + r, p.table, stride=SENT * p.scal), :] for s in range(p.scal)]
+        rows = [recv_ref[pl.ds(s * p.table * SENT + r, p.table, stride=SENT), :] for s in range(p.scal)]
         return jnp.concatenate(rows, axis=0)
 
     addresses = jnp.concatenate([received(4), received(6)], axis=0)
@@ -534,8 +534,8 @@
     )
 
 
-def exchange(array):
-    return lax.all_to_all(array, AXES, split_axis=0, concat_axis=0, tiled=True)
+def exchange(array, axes):
+    return lax.all_to_all(array, axes, split_axis=0, concat_axis=0, tiled=True)
 
 
 def on_device(plan, cell_coords, flamelet_table, owner_shard, local_bin):
@@ -566,7 +566,7 @@
         1 << 20,
         "requests",
     )(*[pltpu.with_memory_space_constraint(a, pltpu.HBM) for a in (cell_coords, owners, bins, table)])
-    received = exchange(requests.reshape(p.devices, 1, SENT * LANES))
+    received = exchange(requests.reshape(p.devices, 1, SENT * LANES), AXES[::-1])
     received = received.reshape(p.devices * SENT, LANES)
     replies, place = call(
         lookup_kernel,
@@ -581,7 +581,7 @@
         1 << 24,
         "lookup",
     )(received, early, pltpu.with_memory_space_constraint(table, pltpu.HBM))
-    answers = exchange(replies.reshape(p.devices, 1, p.rows * LANES))
+    answers = exchange(replies.reshape(p.devices, 1, p.rows * LANES), AXES)
     answers = answers.reshape(p.devices * p.rows, LANES)
 
     filter_op = filter_table(p.nx).T

time: 41 us -> 40.7 us (level)
  no operation moved by 1% of the time
where the time goes in v10:
time: 40.7 us; the launch traced here: 40.4 us
  blocking collectives  28.6 us (70%)
  Pallas kernels  11.2 us (28%)
  between operations  0.65 us (2%)
    all_to_all x2, blocking collectives, exchange(): return lax.all_to_all(array, axes, split_axis=0, concat_axis=0, tiled=True)  28.6 us
    pallas_call x1, Pallas kernels, on_device(): call(lookup_kernel, p, (jax.ShapeDtypeStruct((p.devices * p.rows, LANES),...  7.64 us
    pallas_call x1, Pallas kernels, on_device(): call(request_kernel, p, (jax.ShapeDtypeStruct((p.devices * SENT, LANES),...  1.9 us
    pallas_call x1, Pallas kernels, on_device(): call(filter_kernel, p, (out, out), [VMEM] * 3, [pltpu.VMEM((SCAL_ALL, p.t...  1.68 us

profile of v10, /device:TPU:0, one launch (start us, length us, event | category | flops | bytes accessed | tf_op | source)
XLA Modules:
  0.0 40.4 jit_solution(5339210234817822483)
XLA Ops:
  0.6 1.9 %requests.1 = (f32[224,128]{1,0:T(8,128)S(1)}, f32[5632,128]{1,0:T(8,128)S(1)}) custom-call(f32[4,1024]{1,0:T(4,128)} %coords_in.1, s32[8,128]{1,0:T(8,128)} %bitcast.19, s32[8,128]{1,0:T(8,128)} %bitcast.20, f32[16384,128]{1,0:T(8,128)} %bitcast.17), custom_call_target="tpu_custom_call" | custom-call | flops 1048576 | bytes 4096 | tf_op jit(solution)/shard_map/requests/pallas_call | solution.py:550
  2.5 15.1 %all_to_all.10 = f32[32,1,896]{2,1,0:T(1,128)S(1)} all-to-all(f32[32,1,896]{2,1,0:T(1,128)S(1)} %bitcast.16), channel_id=1, replica_groups=mesh['table'=16,'scal'=2] {'scal','table'}, dimensions={0} | all-to-all | bytes 229376 | tf_op jit(solution)/shard_map/all_to_all | solution.py:538
  17.7 0.0 copy-start
  17.7 7.6 %lookup.1 = (f32[640,128]{1,0:T(8,128)S(1)}, bf16[4,640,256]{2,1,0:T(8,128)(2,1)S(1)}) custom-call(f32[224,128]{1,0:T(8,128)S(1)} %bitcast.14, f32[5632,128]{1,0:T(8,128)S(1)} %get-tuple-element.9.early_ref, f32[16384,128]{1,0:T(8,128)} %bitcast.18), custom_call_target="tpu_custom_call" | custom-call | flops 16777216 | bytes 65536 | tf_op jit(solution)/shard_map/lookup/pallas_call | solution.py:571
  25.3 13.4 %all_to_all.11 = f32[32,1,2560]{2,1,0:T(1,128)S(1)} all-to-all(f32[32,1,2560]{2,1,0:T(1,128)S(1)} %bitcast.15), channel_id=1, replica_groups=mesh['table'=16,'scal'=2] {'table','scal'}, dimensions={0} | all-to-all | bytes 655360 | tf_op jit(solution)/shard_map/all_to_all | solution.py:538
  38.8 0.0 copy-done
  38.8 1.7 %filter.1 = (f32[256,128]{1,0:T(8,128)}, f32[256,128]{1,0:T(8,128)}) custom-call(f32[640,128]{1,0:T(8,128)S(1)} %bitcast.13, bf16[4,640,256]{2,1,0:T(8,128)(2,1)S(1)} %get-tuple-element.11.place_ref, f32[128,256]{1,0:T(8,128)S(1)} %copy-done), custom_call_target="tpu_custom_call" | custom-call | flops 16777216 | bytes 65536 | tf_op jit(solution)/shard_map/filter/pallas_call | solution.py:591
Async XLA Ops:
  17.7 21.1 %copy-start = (f32[128,256]{1,0:T(8,128)S(1)}, f32[128,256]{1,0:T(8,128)}, u32[]{:S(2)}) copy-start(f32[128,256]{1,0:T(8,128)} %constant.2.clone.op_ref) | copy-start | bytes 393220

commit v11 on v10

--- a/solution.py
+++ b/solution.py
@@ -484,11 +484,9 @@
             put(tiles, sc * p.scalars, (p.table // 4 + quad // 4) * LANES)
     sides = []
     for h in range(4):
-        left = jnp.concatenate(pieces_of(left_refs[h][...], 3), axis=0)
+        left = jnp.concatenate(pieces_of(left_refs[h][...], 2), axis=0)
         values = jnp.dot(left, place_ref[h], preferred_element_type=jnp.float32)
-        sides.append(
-            values[0:SCAL_ALL] + values[SCAL_ALL : 2 * SCAL_ALL] + values[2 * SCAL_ALL :]
-        )
+        sides.append(values[:SCAL_ALL] + values[SCAL_ALL:])
     part_x = p.nx // 4
     if part_x == 32:
         lines = []

time: 40.7 us -> 40.6 us (level)
  no operation moved by 1% of the time
where the time goes in v11:
time: 40.6 us; the launch traced here: 40.4 us
  blocking collectives  28.6 us (70%)
  Pallas kernels  11.2 us (28%)
  between operations  0.65 us (2%)
    all_to_all x2, blocking collectives, exchange(): return lax.all_to_all(array, axes, split_axis=0, concat_axis=0, tiled=True)  28.6 us
    pallas_call x1, Pallas kernels, on_device(): call(lookup_kernel, p, (jax.ShapeDtypeStruct((p.devices * p.rows, LANES),...  7.68 us
    pallas_call x1, Pallas kernels, on_device(): call(request_kernel, p, (jax.ShapeDtypeStruct((p.devices * SENT, LANES),...  1.9 us
    pallas_call x1, Pallas kernels, on_device(): call(filter_kernel, p, (out, out), [VMEM] * 3, [pltpu.VMEM((SCAL_ALL, p.t...  1.61 us

profile of v11, /device:TPU:0, one launch (start us, length us, event | category | flops | bytes accessed | tf_op | source)
XLA Modules:
  0.0 40.4 jit_solution(18100115810932300149)
XLA Ops:
  0.6 1.9 %requests.1 = (f32[224,128]{1,0:T(8,128)S(1)}, f32[5632,128]{1,0:T(8,128)S(1)}) custom-call(f32[4,1024]{1,0:T(4,128)} %coords_in.1, s32[8,128]{1,0:T(8,128)} %bitcast.19, s32[8,128]{1,0:T(8,128)} %bitcast.20, f32[16384,128]{1,0:T(8,128)} %bitcast.17), custom_call_target="tpu_custom_call" | custom-call | flops 1048576 | bytes 4096 | tf_op jit(solution)/shard_map/requests/pallas_call | solution.py:548
  2.5 15.1 %all_to_all.10 = f32[32,1,896]{2,1,0:T(1,128)S(1)} all-to-all(f32[32,1,896]{2,1,0:T(1,128)S(1)} %bitcast.16), channel_id=1, replica_groups=mesh['table'=16,'scal'=2] {'scal','table'}, dimensions={0} | all-to-all | bytes 229376 | tf_op jit(solution)/shard_map/all_to_all | solution.py:536
  17.7 0.0 copy-start
  17.7 7.7 %lookup.1 = (f32[640,128]{1,0:T(8,128)S(1)}, bf16[4,640,256]{2,1,0:T(8,128)(2,1)S(1)}) custom-call(f32[224,128]{1,0:T(8,128)S(1)} %bitcast.14, f32[5632,128]{1,0:T(8,128)S(1)} %get-tuple-element.9.early_ref, f32[16384,128]{1,0:T(8,128)} %bitcast.18), custom_call_target="tpu_custom_call" | custom-call | flops 16777216 | bytes 65536 | tf_op jit(solution)/shard_map/lookup/pallas_call | solution.py:569
  25.4 13.4 %all_to_all.11 = f32[32,1,2560]{2,1,0:T(1,128)S(1)} all-to-all(f32[32,1,2560]{2,1,0:T(1,128)S(1)} %bitcast.15), channel_id=1, replica_groups=mesh['table'=16,'scal'=2] {'table','scal'}, dimensions={0} | all-to-all | bytes 655360 | tf_op jit(solution)/shard_map/all_to_all | solution.py:536
  38.8 0.0 copy-done
  38.8 1.6 %filter.1 = (f32[256,128]{1,0:T(8,128)}, f32[256,128]{1,0:T(8,128)}) custom-call(f32[640,128]{1,0:T(8,128)S(1)} %bitcast.13, bf16[4,640,256]{2,1,0:T(8,128)(2,1)S(1)} %get-tuple-element.11.place_ref, f32[128,256]{1,0:T(8,128)S(1)} %copy-done), custom_call_target="tpu_custom_call" | custom-call | flops 16777216 | bytes 65536 | tf_op jit(solution)/shard_map/filter/pallas_call | solution.py:589
Async XLA Ops:
  17.7 21.1 %copy-start = (f32[128,256]{1,0:T(8,128)S(1)}, f32[128,256]{1,0:T(8,128)}, u32[]{:S(2)}) copy-start(f32[128,256]{1,0:T(8,128)} %constant.2.clone.op_ref) | copy-start | bytes 393220

commit v12 on v11

--- a/solution.py
+++ b/solution.py
@@ -419,7 +419,7 @@
 
     for g in range(p.table):
         for s in range(p.scal):
-            dest, chunk = g * p.scal + s, s * p.table + g
+            dest = chunk = s * p.table + g
             out_ref[dest * p.rows : dest * p.rows + p.scalars, :] = tile_ref[
                 chunk * p.scalars : (chunk + 1) * p.scalars, :
             ]
@@ -439,7 +439,7 @@
                     message = jnp.where(
                         quad_of == b, moved[b * p.few : (b + 1) * p.few], message
                     )
-                start = ((quad * 4 + i) * p.scal + s) * p.rows + p.scalars
+                start = (s * p.table + quad * 4 + i) * p.rows + p.scalars
                 out_ref[start : start + p.few, :] = message
 
 
@@ -464,13 +464,13 @@
 
     for sc in range(p.scal):
         for o in range(0, p.table, 4):
-            starts = [((o + i) * p.scal + sc) * p.rows for i in range(4)]
+            starts = [(sc * p.table + o + i) * p.rows for i in range(4)]
             tiles = [recv_ref[start : start + p.scalars, :] for start in starts]
             put(tiles, sc * p.scalars, o // 4 * LANES)
         for quad in range(0, p.table // 4, 4):
             tiles = []
             for n in range(4):
-                starts = [((quad + n) * 4 + i) * p.scal + sc for i in range(4)]
+                starts = [sc * p.table + (quad + n) * 4 + i for i in range(4)]
                 starts = [start * p.rows + p.scalars for start in starts]
                 tile = []
                 for b in range(4):
@@ -579,7 +579,7 @@
         1 << 24,
         "lookup",
     )(received, early, pltpu.with_memory_space_constraint(table, pltpu.HBM))
-    answers = exchange(replies.reshape(p.devices, 1, p.rows * LANES), AXES)
+    answers = exchange(replies.reshape(p.devices, 1, p.rows * LANES), AXES[::-1])
     answers = answers.reshape(p.devices * p.rows, LANES)
 
     filter_op = filter_table(p.nx).T

time: 40.6 us -> 40.6 us (level)
  no operation moved by 1% of the time
where the time goes in v12:
time: 40.6 us; the launch traced here: 40.4 us
  blocking collectives  28.5 us (70%)
  Pallas kernels  11.2 us (28%)
  between operations  0.65 us (2%)
    all_to_all x2, blocking collectives, exchange(): return lax.all_to_all(array, axes, split_axis=0, concat_axis=0, tiled=True)  28.5 us
    pallas_call x1, Pallas kernels, on_device(): call(lookup_kernel, p, (jax.ShapeDtypeStruct((p.devices * p.rows, LANES),...  7.66 us
    pallas_call x1, Pallas kernels, on_device(): call(request_kernel, p, (jax.ShapeDtypeStruct((p.devices * SENT, LANES),...  1.9 us
    pallas_call x1, Pallas kernels, on_device(): call(filter_kernel, p, (out, out), [VMEM] * 3, [pltpu.VMEM((SCAL_ALL, p.t...  1.6 us

profile of v12, /device:TPU:0, one launch (start us, length us, event | category | flops | bytes accessed | tf_op | source)
XLA Modules:
  0.0 40.4 jit_solution(17351608070809944510)
XLA Ops:
  0.6 1.9 %requests.1 = (f32[224,128]{1,0:T(8,128)S(1)}, f32[5632,128]{1,0:T(8,128)S(1)}) custom-call(f32[4,1024]{1,0:T(4,128)} %coords_in.1, s32[8,128]{1,0:T(8,128)} %bitcast.19, s32[8,128]{1,0:T(8,128)} %bitcast.20, f32[16384,128]{1,0:T(8,128)} %bitcast.17), custom_call_target="tpu_custom_call" | custom-call | flops 1048576 | bytes 4096 | tf_op jit(solution)/shard_map/requests/pallas_call | solution.py:548
  2.5 15.1 %all_to_all.10 = f32[32,1,896]{2,1,0:T(1,128)S(1)} all-to-all(f32[32,1,896]{2,1,0:T(1,128)S(1)} %bitcast.16), channel_id=1, replica_groups=mesh['table'=16,'scal'=2] {'scal','table'}, dimensions={0} | all-to-all | bytes 229376 | tf_op jit(solution)/shard_map/all_to_all | solution.py:536
  17.7 0.0 copy-start
  17.7 7.7 %lookup.1 = (f32[640,128]{1,0:T(8,128)S(1)}, bf16[4,640,256]{2,1,0:T(8,128)(2,1)S(1)}) custom-call(f32[224,128]{1,0:T(8,128)S(1)} %bitcast.14, f32[5632,128]{1,0:T(8,128)S(1)} %get-tuple-element.9.early_ref, f32[16384,128]{1,0:T(8,128)} %bitcast.18), custom_call_target="tpu_custom_call" | custom-call | flops 16777216 | bytes 65536 | tf_op jit(solution)/shard_map/lookup/pallas_call | solution.py:569
  25.3 13.4 %all_to_all.11 = f32[32,1,2560]{2,1,0:T(1,128)S(1)} all-to-all(f32[32,1,2560]{2,1,0:T(1,128)S(1)} %bitcast.15), channel_id=1, replica_groups=mesh['table'=16,'scal'=2] {'scal','table'}, dimensions={0} | all-to-all | bytes 655360 | tf_op jit(solution)/shard_map/all_to_all | solution.py:536
  38.7 0.0 copy-done
  38.8 1.6 %filter.1 = (f32[256,128]{1,0:T(8,128)}, f32[256,128]{1,0:T(8,128)}) custom-call(f32[640,128]{1,0:T(8,128)S(1)} %bitcast.13, bf16[4,640,256]{2,1,0:T(8,128)(2,1)S(1)} %get-tuple-element.11.place_ref, f32[128,256]{1,0:T(8,128)S(1)} %copy-done), custom_call_target="tpu_custom_call" | custom-call | flops 16777216 | bytes 65536 | tf_op jit(solution)/shard_map/filter/pallas_call | solution.py:589
Async XLA Ops:
  17.7 21.1 %copy-start = (f32[128,256]{1,0:T(8,128)S(1)}, f32[128,256]{1,0:T(8,128)}, u32[]{:S(2)}) copy-start(f32[128,256]{1,0:T(8,128)} %constant.2.clone.op_ref) | copy-start | bytes 393220
